TPU v7x, 32 devices: a whole 2x2x4 slice. The times are simulated.
32 devices in a mesh: dp: 8 (over y, x, core), tensor: 4 (over z).
Axes of the slice: x: 2, y: 2, z: 4, core: 2. Of those that a mesh axis runs over, the one named last changes fastest.
Arguments:
- tokens: bfloat16 [8192, 2048], P(('dp', 'tensor')), may hold values from -6 to 6
- segments: int32 [8192], P('dp'), may hold values from 0 to 2, as said below
- positions: int32 [8192], P('dp'), may hold values from 0 to 2047, as said below
- attn_gain: bfloat16 [2048], P('dp'), may hold values from 0.099609375 to 1.8984375
- w_query: bfloat16 [2048, 2048], P('dp', 'tensor'), may hold values from -0.125 to 0.125
- w_key: bfloat16 [2048, 512], P('dp', 'tensor'), may hold values from -0.125 to 0.125
- w_value: bfloat16 [2048, 512], P('dp', 'tensor'), may hold values from -0.125 to 0.125
- w_out: bfloat16 [2048, 2048], P('tensor', 'dp'), may hold values from -1.5 to 1.5
- mlp_gain: bfloat16 [2048], P('dp'), may hold values from 0.099609375 to 1.8984375
- w_gate: bfloat16 [2048, 8192], P('dp', 'tensor'), may hold values from -0.125 to 0.125
- w_up: bfloat16 [2048, 8192], P('dp', 'tensor'), may hold values from -0.125 to 0.125
- w_down: bfloat16 [8192, 2048], P('tensor', 'dp'), may hold values from -0.0625 to 0.0625
- grad_out: bfloat16 [8192, 2048], P(('dp', 'tensor')), may hold values from -6 to 6
Outputs:
- block_out: bfloat16 [8192, 2048], P(('dp', 'tensor'))
- grad_tokens: float32 [8192, 2048], P(('dp', 'tensor'))
- grad_attn_gain: float32 [2048], P('dp')
- grad_query: float32 [2048, 2048], P('dp', 'tensor')
- grad_key: float32 [2048, 512], P('dp', 'tensor')
- grad_value: float32 [2048, 512], P('dp', 'tensor')
- grad_out_proj: float32 [2048, 2048], P('tensor', 'dp')
- grad_mlp_gain: float32 [2048], P('dp')
- grad_gate: float32 [2048, 8192], P('dp', 'tensor')
- grad_up: float32 [2048, 8192], P('dp', 'tensor')
- grad_down: float32 [8192, 2048], P('tensor', 'dp')
Inputs may be any that keep to these rules, and one draw needn't show every extreme that they name: `segments`: each sequence of 1024 tokens holds three documents numbered 0, 1, 2 in order: document 0 ends before token 256 and document 1 ends after token 768 and at least 64 tokens before the sequence's end. Within a document positions rise by one from token to token; each document's first position is below 2048.
All inputs are finite; a program needn't handle non-finite values.
Results may differ from a plain program's by a relative error of at most 0.013.
Values may be sent and summed in bfloat16 or wider, within the bound.
A program may use at most 256 MiB of HBM per device.

v0:
```python
import functools
import math

import jax
import jax.numpy as jnp
from jax import lax
from jax.experimental import pallas as pl
from jax.experimental.pallas import tpu as pltpu
from jax.sharding import PartitionSpec as P

HD = 64
EPSILON = 1e-05
MASKED = -1e30
F32 = jnp.float32
BF = jnp.bfloat16

def turn_t(values, cosine, sine, sign):
    half=values.shape[0]//2
    first, second = values[:half], values[half:]
    return jnp.concatenate([first*cosine - sign*second*sine, second*cosine + sign*first*sine],0)

def column(row_ref):
    return jnp.broadcast_to(row_ref[...].astype(F32),(8,row_ref.shape[1])).T[:,0:1].astype(jnp.int32)

def block_bias(segs_col, segs_row, start, block):
    keys=start+block
    key_places=lax.broadcasted_iota(jnp.int32,(keys,block),0)
    query_places=start+lax.broadcasted_iota(jnp.int32,(keys,block),1)
    allowed=(key_places<=query_places)&(segs_col[0:keys,:]==segs_row[0:1,start:start+block])
    return jnp.where(allowed,0.0,MASKED).astype(F32)

def attend_kernel(heads, groups, block, count, pieces, fine, mix_hbm, normed_hbm, cos_ref, sin_ref, segr_ref, wo_hbm, grad_ref, tokens_hbm, gain_ref,
                  mixed_ref, lse_ref, q_ref, kt_ref, k_ref, v_ref, residual_ref, rows_hbm, whole_hbm,
                  mix_ref, normed_ref, lin_ref, bias_ref, vt_ref, wo_ref, tokens_ref, part_ref, held, hs, hr, sums, total, ss, sr, moved, ms, mr, cs):
    length=normed_ref.shape[0]
    per=heads//groups
    rows=grad_ref.shape[0]
    early=held.shape[1]
    line=Line(count,pieces,rows,held=held,held_sems=(hs,hr),sub=early//pieces)
    inputs=[pltpu.make_async_copy(s,d,cs.at[4+k]) for k,(s,d) in enumerate(((normed_hbm,normed_ref),(mix_hbm,mix_ref)))]
    for copy in inputs: copy.start()
    greet(line.here,count)
    line.gather_step(0,grad_ref)
    for copy in inputs: copy.wait()
    weights=pltpu.make_async_copy(wo_hbm,wo_ref,cs.at[0])
    weights.start()
    stream=pltpu.make_async_copy(tokens_hbm,tokens_ref,cs.at[1])
    stream.start()
    lines=mix_ref.shape[1]
    cut=256 if lines%256==0 else lines
    for c in range(0,lines,cut):
        lin_ref[c:c+cut,:]=lax.dot_general(mix_ref[:,c:c+cut],normed_ref[...],(((0,),(1,)),((),())),preferred_element_type=F32)
    steps=line.gather_steps()
    done=0
    def tick():
        nonlocal done
        if done+1<steps:
            done+=1
            line.gather_step(done,grad_ref)
    tick()
    cosine, sine = cos_ref[...], sin_ref[...]
    def rope(h,_):
        rows=pl.ds(pl.multiple_of(h*HD,HD),HD)
        q_ref[rows,:]=(turn_t(lin_ref[rows,:],cosine,sine,1.0).astype(BF)*jnp.asarray(0.125,BF))
        return 0
    lax.fori_loop(0,heads,rope,0)
    turned=[turn_t(lin_ref[(heads+g)*HD:(heads+g+1)*HD,:],cosine,sine,1.0) for g in range(groups)]
    keys_t=jnp.concatenate(turned,0)
    kt_ref[...]=keys_t.astype(BF)
    vals_t=lin_ref[(heads+groups)*HD:(heads+2*groups)*HD,:]
    vt_ref[...]=vals_t.astype(BF)
    keys_n=keys_t.T.astype(BF)
    vals_n=vals_t.T.astype(BF)
    for g in range(groups):
        k_ref[g]=keys_n[:,g*HD:(g+1)*HD]
        v_ref[g]=vals_n[:,g*HD:(g+1)*HD]
    segs_col=column(segr_ref)
    for start in range(0,length,block):
        keys=start+block
        if start in (block,3*block): tick()
        bias_ref[0:keys,:]=block_bias(segs_col,segr_ref,start,block)
        def head(h,_):
            g=h//per
            rows=pl.ds(pl.multiple_of(h*HD,HD),HD)
            grows=pl.ds(pl.multiple_of(g*HD,HD),HD)
            scores=jnp.dot(k_ref[g,0:keys,:],q_ref[rows,start:start+block],preferred_element_type=F32)
            scores=scores+bias_ref[0:keys,:]
            top=jnp.max(scores,0,keepdims=True)
            weights=jnp.exp(scores-top)
            total=jnp.sum(weights,0,keepdims=True)
            out=jnp.dot(vt_ref[grows,0:keys],weights.astype(BF),preferred_element_type=F32)
            mixed_ref[rows,start:start+block]=(out/total).astype(BF)
            lse_ref[h,:,start:start+block]=top+jnp.log(total)
            return 0
        lax.fori_loop(0,heads,head,0)
    width=wo_ref.shape[1]
    wide=min(512,width)
    weights.wait()
    tick()
    def out(c,_):
        cols=pl.ds(pl.multiple_of(c*wide,wide),wide)
        product=lax.dot_general(mixed_ref[...],wo_ref[:,cols],(((0,),(0,)),((),())),preferred_element_type=F32).astype(BF)
        for j in range(count): part_ref[j,:,cols]=product[j*rows:(j+1)*rows]
        return 0
    lax.fori_loop(0,width//wide,out,0)
    held[line.here]=grad_ref[0:early,:]
    copy=pltpu.make_async_copy(held,rows_hbm,cs.at[2])
    stream.wait()
    sweep=Line(count,fine,rows,part_ref,sums,(ss,sr),moved,(ms,mr))
    def finish(span,total):
        residual=total[...]+tokens_ref[span,:].astype(F32)
        residual_ref[span,:]=residual
        scale=lax.rsqrt(jnp.mean(residual*residual,-1,keepdims=True)+EPSILON)
        return (residual*scale*gain_ref[1:2,:]).astype(BF)
    def step(t,_):
        sweep.sweep(t,total,finish)
        for k in range(done+1,steps):
            @pl.when(t==2*(k-done-1))
            def _(): line.gather_step(k,grad_ref)
        return 0
    lax.fori_loop(0,sweep.sweep_steps(),step,0)
    copy.start()
    last=pltpu.make_async_copy(moved,whole_hbm,cs.at[3])
    last.start()
    line.end_pieces()
    sweep.end_sums()
    sweep.end_pieces()
    copy.wait()
    last.wait()

def attend(mix, normed, cosine, sine, segments, w_out, grad_out, tokens, gain, heads, groups, cid, early, pieces, fine, count):
    length,width=normed.shape
    rows=grad_out.shape[0]
    block=min(256,length)
    sds=jax.ShapeDtypeStruct
    vm=pl.BlockSpec(memory_space=pltpu.VMEM)
    hbm=pl.BlockSpec(memory_space=pl.ANY)
    sem=pltpu.SemaphoreType.DMA
    vmem=pltpu.VMEM
    return pl.pallas_call(functools.partial(attend_kernel,heads,groups,block,count,pieces,fine),
        out_shape=(sds((heads*HD,length),BF),sds((heads,1,length),F32),sds((heads*HD,length),BF),
            sds((groups*HD,length),BF),sds((groups,length,HD),BF),sds((groups,length,HD),BF),
            sds((rows,width),F32),sds((count,early,width),BF),sds((count,rows,width),BF)),
        in_specs=[hbm,hbm]+[vm]*3+[hbm,vm,hbm,vm],out_specs=(vm,)*7+(hbm,hbm),
        scratch_shapes=[vmem(mix.shape,BF),vmem(normed.shape,BF),vmem((mix.shape[1],length),F32),vmem((length,block),F32),vmem((groups*HD,length),BF),vmem(w_out.shape,BF),
            vmem(tokens.shape,BF),vmem((count,rows,width),BF),vmem((count,early,width),BF),sem((2,count,pieces)),sem((2,count,pieces)),
            vmem((count+1,rows,width),BF),vmem((rows//fine,width),F32),sem((2,count,fine)),sem((2,count,fine)),
            vmem((count,rows,width),BF),sem((2,count,fine)),sem((2,count,fine)),sem((6,))],
        cost_estimate=pl.CostEstimate(flops=30_000_000_000,bytes_accessed=500_000_000,transcendentals=8_000_000),
        compiler_params=pltpu.CompilerParams(collective_id=cid,has_side_effects=True,vmem_limit_bytes=58*1024*1024),
    )(mix,normed,cosine,sine,segments.reshape(1,length),w_out,grad_out,tokens,gain)

def attend_back_kernel(heads, groups, block, count, pieces, fine, grads_hbm, two_hbm, go_ref, gain_ref, wo_hbm, q_ref, kt_ref, k_ref, v_ref, lse_ref, cos_ref, sin_ref, segr_ref,
                  down_ref, res_ref, early_ref, mixed_hbm, normed_hbm, mix_hbm,
                  gres_ref, acc, part_hbm, grad_hbm, out_ref,
                  part_ref, normed_ref, low_ref, wide_sums, wide_total, ws, wr, hs, hr,
                  wo_ref, mixed_ref, mix_ref, turn_ref, gm_ref, bias_ref, qn_ref, gn_ref, dq_ref, dk_ref, dv_ref, sums, total, ss, sr, grad_ref, cs, gs_sem):
    length=q_ref.shape[1]
    per=heads//groups
    width=wo_ref.shape[1]
    rows=res_ref.shape[0]
    half=rows//2
    line=Line(count,pieces,half,down_ref,sums,(ss,sr))
    sweep=Line(count,fine,rows,part_ref,wide_sums,(ws,wr),low_ref,(hs,hr))
    first=pltpu.make_async_copy(grads_hbm,part_ref,cs.at[0])
    first.start()
    second=pltpu.make_async_copy(two_hbm,normed_ref,cs.at[1])
    second.start()
    late=[pltpu.make_async_copy(s,d,cs.at[2+k]) for k,(s,d) in enumerate(((mixed_hbm,mixed_ref),(mix_hbm,mix_ref),(wo_hbm,wo_ref)))]
    for copy in late: copy.start()
    greet(line.here,count)
    acc[...]=jnp.zeros_like(acc)
    out_ref[0:half,:]=early_ref[...]
    first.wait()
    def turn(span,total):
        residual=res_ref[span,:]
        scale=lax.rsqrt(jnp.mean(residual*residual,-1,keepdims=True)+EPSILON)
        unit=residual*scale
        scaled=total[...]*gain_ref[1:2,:]
        grads=go_ref[span,:].astype(F32)+scale*(scaled-unit*jnp.mean(scaled*unit,-1,keepdims=True))
        gres_ref[span,:]=grads
        return grads.astype(BF)
    def finish(span,total):
        places=pl.ds(pl.multiple_of(half+span.start,line.sub),line.sub)
        out_ref[places,:]=(res_ref[places,:]+total[...]).astype(BF)
    steps=sweep.sweep_steps()
    begun=2
    def step(t,_):
        sweep.sweep(t,wide_total,turn)
        @pl.when(t==2)
        def _(): second.wait()
        @pl.when((t>=2)&(t<count+2))
        def _(): gain_terms(part_ref,normed_ref,acc,jnp.clip(t-2,0,count-1))
        for k in range(begun):
            @pl.when(t==steps-2*(begun-k))
            def _(): line.far_step(jnp.int32(k),total,finish)
        return 0
    lax.fori_loop(0,steps,step,0)
    third=pltpu.make_async_copy(normed_hbm,normed_ref,cs.at[1])
    third.start()
    ticks=[begun]
    def tick(amount=1):
        for _ in range(amount):
            if ticks[0]<line.far_steps():
                line.far_step(jnp.int32(ticks[0]),total,finish)
                ticks[0]+=1
    late[2].wait()
    whole=lambda: low_ref[...].reshape(length,width)
    cosine, sine = cos_ref[...], sin_ref[...]
    deep=heads*HD
    cut=256 if deep%256==0 else deep
    for c in range(0,deep,cut):
        gm_ref[c:c+cut,:]=lax.dot_general(wo_ref[c:c+cut,:],whole(),(((1,),(1,)),((),())),preferred_element_type=F32).astype(BF)
    def flip(p,_):
        rows=pl.ds(pl.multiple_of(p*2*HD,2*HD),2*HD)
        qn=q_ref[rows,:].astype(F32).T.astype(BF)
        gn=gm_ref[rows,:].astype(F32).T.astype(BF)
        qn_ref[2*p]=qn[:,:HD]
        qn_ref[2*p+1]=qn[:,HD:]
        gn_ref[2*p]=gn[:,:HD]
        gn_ref[2*p+1]=gn[:,HD:]
        return 0
    lax.fori_loop(0,heads//2,flip,0)
    dk_ref[...]=jnp.zeros_like(dk_ref)
    dv_ref[...]=jnp.zeros_like(dv_ref)
    lines=(heads+2*groups)*HD
    strip=min(512,width)
    late[0].wait()
    tick()
    for c in range(0,width,strip):
        grad_ref[c:c+strip,lines:]=lax.dot_general(low_ref[:,:,c:c+strip].reshape(length,strip),mixed_ref[...],(((0,),(1,)),((),())),preferred_element_type=F32).astype(BF)
    segs_col=column(segr_ref)
    for start in range(0,length,block):
        keys=start+block
        cols=slice(start,start+block)
        bias_ref[0:keys,:]=block_bias(segs_col,segr_ref,start,block)
        def head(h,_):
            g=h//per
            rows=pl.ds(pl.multiple_of(h*HD,HD),HD)
            grows=pl.ds(pl.multiple_of(g*HD,HD),HD)
            scores=jnp.dot(k_ref[g,0:keys,:],q_ref[rows,cols],preferred_element_type=F32)
            probs=jnp.exp(scores+bias_ref[0:keys,:]-lse_ref[h,:,cols])
            dv_ref[g,0:keys,:]+=jnp.dot(probs.astype(BF),gn_ref[h,cols,:],preferred_element_type=F32)
            gp=jnp.dot(v_ref[g,0:keys,:],gm_ref[rows,cols],preferred_element_type=F32)
            weighted=probs*gp
            centre=jnp.sum(weighted,0,keepdims=True)
            gs=(weighted-probs*centre).astype(BF)
            dk_ref[g,0:keys,:]+=jnp.dot(gs,qn_ref[h,cols,:],preferred_element_type=F32)
            dq_ref[rows,cols]=0.125*jnp.dot(kt_ref[grows,0:keys],gs,preferred_element_type=F32)
            return 0
        lax.fori_loop(0,heads,head,0)
        if start>0: tick()
    def back(h,_):
        rows=pl.ds(pl.multiple_of(h*HD,HD),HD)
        turn_ref[rows,:]=turn_t(dq_ref[rows,:],cosine,sine,-1.0).astype(BF)
        return 0
    lax.fori_loop(0,heads,back,0)
    dk=jnp.concatenate([dk_ref[g] for g in range(groups)],1).T
    dv=jnp.concatenate([dv_ref[g] for g in range(groups)],1).T
    for g in range(groups):
        turn_ref[(heads+g)*HD:(heads+g+1)*HD,:]=turn_t(dk[g*HD:(g+1)*HD],cosine,sine,-1.0).astype(BF)
    turn_ref[(heads+groups)*HD:,:]=dv.astype(BF)
    late[1].wait()
    sweep.end_sums()
    for c in range(0,width,strip):
        product=lax.dot_general(turn_ref[...],mix_ref[c:c+strip,:],(((0,),(1,)),((),())),preferred_element_type=F32).astype(BF)
        for j in range(count): part_ref[j,:,c:c+strip]=product[j*rows:(j+1)*rows]
    give=pltpu.make_async_copy(part_ref,part_hbm,cs.at[0])
    give.start()
    tick()
    third.wait()
    for k,c in enumerate(range(0,width,strip)):
        grad_ref[c:c+strip,0:lines]=lax.dot_general(normed_ref[:,:,c:c+strip].reshape(length,strip),turn_ref[...],(((0,),(1,)),((),())),preferred_element_type=F32).astype(BF)
        pltpu.make_async_copy(grad_ref.at[c:c+strip],grad_hbm.at[c:c+strip],gs_sem.at[k]).start()
    tick(line.far_steps())
    line.end_sums()
    sweep.end_pieces()
    give.wait()
    for k,c in enumerate(range(0,width,strip)):
        pltpu.make_async_copy(grad_ref.at[c:c+strip],grad_hbm.at[c:c+strip],gs_sem.at[k]).wait()

def attend_back(grads,two,grad_out,gain,w_out,q,kt,k,v,lse,cosine,sine,segments,down,residual,early,mixed,normed,mix,heads,groups,cid,pieces,fine,count):
    rows,width=residual.shape
    length=rows*count
    lines=mix.shape[1]
    block=min(256,length)
    vm=pl.BlockSpec(memory_space=pltpu.VMEM)
    hbm=pl.BlockSpec(memory_space=pl.ANY)
    vmem=pltpu.VMEM
    sds=jax.ShapeDtypeStruct
    sem=pltpu.SemaphoreType.DMA
    cut=lambda x: x.reshape(count,rows,width)
    return pl.pallas_call(functools.partial(attend_back_kernel,heads,groups,block,count,pieces,fine),
        out_shape=(sds((rows,width),F32),sds((8,width),F32),sds((count,rows,width),BF),sds((width,lines+heads*HD),BF),sds((rows,width),BF)),
        in_specs=[hbm,hbm,vm,vm,hbm]+[vm]*11+[hbm]*3,out_specs=(vm,vm,hbm,hbm,vm),
        scratch_shapes=[vmem((count,rows,width),BF),vmem((count,rows,width),BF),vmem((count,rows,width),BF),vmem((count+1,rows,width),BF),
            vmem((rows//fine,width),F32),sem((2,count,fine)),sem((2,count,fine)),sem((2,count,fine)),sem((2,count,fine)),
            vmem(w_out.shape,BF),vmem(mixed.shape,BF),vmem(mix.shape,BF),vmem((lines,length),BF),vmem((heads*HD,length),BF),
            vmem((length,block),F32),vmem((heads,length,HD),BF),vmem((heads,length,HD),BF),
            vmem((heads*HD,length),F32),vmem((groups,length,HD),F32),vmem((groups,length,HD),F32),
            vmem((count+1,rows//2,width),BF),vmem((rows//2//pieces,width),F32),sem((2,count,pieces)),sem((2,count,pieces)),
            vmem((width,lines+heads*HD),BF),sem((5,)),sem((max(1,width//min(512,width)),))],
        cost_estimate=pl.CostEstimate(flops=60_000_000_000,bytes_accessed=550_000_000,transcendentals=8_000_000),
        compiler_params=pltpu.CompilerParams(collective_id=cid,has_side_effects=True,vmem_limit_bytes=60*1024*1024),
    )(cut(grads),cut(two),grad_out,gain,w_out,q,kt,k,v,lse,cosine,sine,segments.reshape(1,length),down,residual,early,mixed,cut(normed),mix)


AXIS="tensor"
DP="dp"
MESH=pl.DeviceIdType.MESH

def greet(here, count, plane=0):
    barrier=pltpu.get_barrier_semaphore()
    if plane:
        def call(k,_):
            pl.semaphore_signal(barrier,inc=1,device_id={DP:lax.rem(lax.axis_index(DP)+k,plane)},device_id_type=MESH)
            return 0
        lax.fori_loop(1,plane,call,0)
        for k in range(1,count):
            pl.semaphore_signal(barrier,inc=1,device_id={AXIS:lax.rem(here+k,count)},device_id_type=MESH)
        pl.semaphore_wait(barrier,plane+count-2)
    else:
        @pl.when(here>0)
        def _(): pl.semaphore_signal(barrier,inc=1,device_id={AXIS:here-1},device_id_type=MESH)
        @pl.when(here<count-1)
        def _(): pl.semaphore_signal(barrier,inc=1,device_id={AXIS:here+1},device_id_type=MESH)
        pl.semaphore_wait(barrier,jnp.where((here>0)&(here<count-1),2,1))

def swap(axis, count, source, landing, sends, recvs):
    me=lax.axis_index(axis)
    def copy(peer, slot, k):
        return pltpu.make_async_remote_copy(src_ref=source(peer),dst_ref=landing.at[slot],send_sem=sends.at[k],
            recv_sem=recvs.at[slot],device_id={axis:peer},device_id_type=MESH)
    def begin(k,_):
        copy(lax.rem(me+k,count),me,k).start()
        return 0
    def end(k,_):
        peer=lax.rem(me+k,count)
        copy(peer,peer,k).wait_recv()
        copy(peer,me,k).wait_send()
        return 0
    return (lambda: lax.fori_loop(1,count,begin,0)),(lambda: lax.fori_loop(1,count,end,0))

def remote(src,dst,send,recv,target):
    return pltpu.make_async_remote_copy(src_ref=src,dst_ref=dst,send_sem=send,recv_sem=recv,
        device_id={AXIS:target},device_id_type=MESH)

class Line:
    def __init__(self,count,pieces,rows,part=None,sums=None,sum_sems=None,held=None,held_sems=None,base=0,sub=None):
        self.n,self.pieces,self.rows=count,pieces,rows
        self.sub=rows//pieces if sub is None else sub
        self.base=base
        self.here=lax.axis_index(AXIS)
        self.part,self.sums,self.sum_sems=part,sums,sum_sems
        self.held,self.held_sems=held,held_sems
    def span(self,u): return pl.ds(pl.multiple_of(self.base+u*self.sub,self.sub),self.sub)
    def fits(self,u): return (u>=0)&(u<self.pieces)
    def _target(self,way):
        return lax.min(self.here+1,self.n-1) if way==0 else lax.max(self.here-1,0)
    def slot(self,way,j,device):
        return j if way==0 else jnp.where(j==device,self.n,j)
    def sum_copy(self,way,j,u,first):
        sends,recvs=self.sum_sems
        dst=self.sums.at[self.slot(way,j,self._target(way)),self.span(u)]
        src=self.part.at[j,self.span(u)] if first else self.sums.at[self.slot(way,j,self.here),self.span(u)]
        return remote(src,dst,sends.at[way,j,u],recvs.at[way,j,u],self._target(way))
    def sum_arrival(self,way,j,u):
        sends,recvs=self.sum_sems
        ref=self.sums.at[self.slot(way,j,self.here),self.span(u)]
        return remote(ref,ref,sends.at[way,j,u],recvs.at[way,j,u],self._target(way))
    def relay(self,way,j,u,begins,passes):
        @pl.when(begins)
        def _(): self.sum_copy(way,j,u,True).start()
        @pl.when(passes)
        def _():
            self.sum_arrival(way,j,u).wait_recv()
            ref=self.sums.at[j,self.span(u)]
            ref[...]=(ref[...].astype(F32)+self.part[j,self.span(u)].astype(F32)).astype(BF)
            self.sum_copy(way,j,u,False).start()
    def far_steps(self): return (self.n-1)*self.pieces+1
    def far_step(self,t,total,finish):
        here,n,S=self.here,self.n,self.pieces
        for way in (0,1):
            q=t-here if way==0 else t-(n-1-here)
            ok=(q>=0)&(q<S*(n-1-here if way==0 else here))
            q=jnp.clip(q,0,S*(n-1)-1)
            j=n-1-q//S if way==0 else q//S
            end=(here==0) if way==0 else (here==n-1)
            self.relay(way,j,q%S,ok&end,ok&jnp.logical_not(end))
        u=t-(n-2)*S-1
        @pl.when(self.fits(u))
        def _():
            self.own_sum(u,total)
            finish(self.span(u),total)
    def send_sums(self,t):
        here,n=self.here,self.n
        for k in range(n-1):
            for way,j in ((0,n-1-k),(1,k)):
                u=t-here-(n-1-j) if way==0 else t-(n-1-here)-j
                ok=self.fits(u)
                u=jnp.clip(u,0,self.pieces-1)
                begins=(here==0) if way==0 else (here==n-1)
                passes=((here>0)&(here<j)) if way==0 else ((here<n-1)&(here>j))
                self.relay(way,j,u,ok&begins,ok&passes)
    def sweep_steps(self): return self.pieces+2*(self.n-1)
    def sweep(self,t,total,finish):
        far=self.n-1
        self.send_sums(t)
        u=t-far
        @pl.when(self.fits(u))
        def _():
            self.own_sum(u,total)
            self.held[self.here,self.span(u)]=finish(self.span(u),total)
            self.send_own(u)
        self.pass_pieces(t-far)
    def own_sum(self,u,total):
        here,n=self.here,self.n
        total[...]=self.part[here,self.span(u)].astype(F32)
        for way in (0,1):
            @pl.when(here>0 if way==0 else here<n-1)
            def _():
                self.sum_arrival(way,here,u).wait_recv()
                total[...]+=self.sums[self.slot(way,here,here),self.span(u)].astype(F32)
    def end_sums(self):
        here,n=self.here,self.n
        def one(u,_):
            for k in range(n-1):
                for way,j in ((0,n-1-k),(1,k)):
                    @pl.when((here<j) if way==0 else (here>j))
                    def _(): self.sum_copy(way,j,u,False).wait_send()
            return 0
        lax.fori_loop(0,self.pieces,one,0)
    def piece_copy(self,way,c,u,src=None):
        sends,recvs=self.held_sems
        dst=self.held.at[c,self.span(u)]
        return remote(dst if src is None else src,dst,sends.at[way,c,u],recvs.at[way,c,u],self._target(way))
    def send_own(self,u,src=None):
        here,n=self.here,self.n
        for way in (0,1):
            @pl.when(here<n-1 if way==0 else here>0)
            def _(): self.piece_copy(way,here,u,src).start()
    def gather_step(self,t,source):
        if t==0:
            for u in range(min(2,self.pieces)): self.send_own(u,source.at[self.span(u),:])
        else:
            self.pass_pieces(t)
            if t+1<self.pieces: self.send_own(t+1,source.at[self.span(t+1),:])
    def gather_steps(self): return self.pieces+self.n-1
    def pass_pieces(self,t,use=None):
        here,n=self.here,self.n
        for k in range(1,n):
            u=t-k
            ok=self.fits(u)
            u=jnp.clip(u,0,self.pieces-1)
            for way in (0,1):
                c=here-k if way==0 else here+k
                there=ok&((c>=0) if way==0 else (c<n))
                c=jnp.clip(c,0,n-1)
                @pl.when(there)
                def _(): self.piece_copy(way,c,u).wait_recv()
                @pl.when(there&(here<n-1 if way==0 else here>0))
                def _(): self.piece_copy(way,c,u).start()
                if use is not None:
                    @pl.when(there)
                    def _(): use(c,u)
    def end_pieces(self):
        here,n=self.here,self.n
        def one(u,_):
            for k in range(n):
                for way in (0,1):
                    c=here-k if way==0 else here+k
                    there=(c>=0) if way==0 else (c<n)
                    c=jnp.clip(c,0,n-1)
                    @pl.when(there&(here<n-1 if way==0 else here>0))
                    def _(): self.piece_copy(way,c,u).wait_send()
            return 0
        lax.fori_loop(0,self.pieces,one,0)

def gain_terms(part,other,acc,c):
    rows=part.shape[1]
    def some(k,_):
        span=pl.ds(pl.multiple_of(k*16,16),16)
        both=part[c,span].astype(F32)*other[c,span].astype(F32)
        acc[...]+=both[:8]+both[8:]
        return 0
    lax.fori_loop(0,rows//16,some,0)

def last_kernel(count, plane, pieces, part_hbm, other_hbm, tokens_hbm, grads_hbm, gain, terms, out, shared, part, other, tokens, grads, cs, sums, total, ss, sr, acc, cut, landed, level, stacked, ds, dr, zs, zr):
    width=part.shape[2]
    line=Line(count,pieces,part.shape[1],part,sums,(ss,sr))
    loads=[pltpu.make_async_copy(s,d,cs.at[k]) for k,(s,d) in enumerate(((part_hbm,part),(other_hbm,other),(tokens_hbm,tokens),(grads_hbm,grads)))]
    for load in loads: load.start()
    greet(line.here,count,plane)
    loads[0].wait()
    acc[...]=jnp.zeros_like(acc)
    me=lax.axis_index(DP)
    piece=width//plane
    begin_dp,end_dp=swap(DP,plane,lambda p: cut.at[p],landed,ds,dr)
    begin_z,end_z=swap(AXIS,count,lambda p: level,stacked,zs,zr)
    def finish(span,total):
        stream=tokens[span,:].astype(F32)
        scale=lax.rsqrt(jnp.mean(stream*stream,-1,keepdims=True)+EPSILON)
        unit=stream*scale
        scaled=total[...]*gain[0:1,:]
        out[span,:]=grads[span,:]+scale*(scaled-unit*jnp.mean(scaled*unit,-1,keepdims=True))
    def step(t,_):
        line.far_step(t,total,finish)
        @pl.when(t==0)
        def _():
            for load in loads[1:]: load.wait()
        @pl.when(t<count)
        def _(): gain_terms(part,other,acc,jnp.clip(t,0,count-1))
        @pl.when(t==count-1)
        def _():
            for p in range(plane):
                cut[p,0:8,:]=acc[:,p*piece:(p+1)*piece]
                cut[p,8:16,:]=terms[:,p*piece:(p+1)*piece]
            landed[me]=cut[me]
            begin_dp()
        @pl.when(t==count+1)
        def _():
            end_dp()
            level[...]=jnp.sum(landed[...],0)
            stacked[line.here]=level[...]
            begin_z()
        return 0
    assert line.far_steps()>count+1
    lax.fori_loop(0,line.far_steps(),step,0)
    end_z()
    shared[...]=jnp.sum(stacked[...],0)
    line.end_sums()

def last_sums(part,other,tokens,grads,gains,terms,cid,pieces,n,plane):
    rows,D=tokens.shape
    vm=pl.BlockSpec(memory_space=pltpu.VMEM)
    hbm=pl.BlockSpec(memory_space=pl.ANY)
    sds=jax.ShapeDtypeStruct
    sem=pltpu.SemaphoreType.DMA
    w=D//plane
    return pl.pallas_call(functools.partial(last_kernel,n,plane,pieces),
        out_shape=(sds((rows,D),F32),sds((16,w),F32)),in_specs=[hbm]*4+[vm]*2,out_specs=(vm,vm),
        scratch_shapes=[pltpu.VMEM((n,rows,D),BF),pltpu.VMEM((n,rows,D),BF),pltpu.VMEM((rows,D),BF),pltpu.VMEM((rows,D),F32),sem((4,)),pltpu.VMEM((n+1,rows,D),BF),pltpu.VMEM((rows//pieces,D),F32),sem((2,n,pieces)),sem((2,n,pieces)),pltpu.VMEM((8,D),F32),
            pltpu.VMEM((plane,16,w),F32),pltpu.VMEM((plane,16,w),F32),pltpu.VMEM((16,w),F32),pltpu.VMEM((n,16,w),F32),
            sem((plane,)),sem((plane,)),sem((n,)),sem((n,))],
        cost_estimate=pl.CostEstimate(flops=0,bytes_accessed=270_000_000,transcendentals=0),
        compiler_params=pltpu.CompilerParams(collective_id=cid,has_side_effects=True,vmem_limit_bytes=56*1024*1024),
    )(part.reshape(n,rows,D),other.reshape(n,rows,D),tokens,grads,gains,terms)


def mlp_kernel(count,pieces,tile,x_hbm,grad_ref,res_ref,early_hbm,wgu_hbm,wd_hbm,
        part_ref,wide_ref,out_ref,rest_hbm,x_ref,gr,product,gated,lifted,down,ring,tall,sums,total,hs,hr,ss,sr,ws,ts,ls,rs,xs):
    s=pl.program_id(0)
    length,hidden=product.shape
    width=x_ref.shape[1]
    rows=grad_ref.shape[0]
    half=rows//2
    first,second=hidden//tile,width//tile
    slots=ring.shape[0]
    at_down=first; at_grad=first+second; at_part=2*first+second; at_weight=2*first+2*second
    begun=early_hbm.shape[1]
    spread=hs.shape[2]
    get=Line(count,spread,rows,held=gr,held_sems=(hs,hr),base=begun,sub=(rows-begun)//spread)
    line=Line(count,pieces,rows,down,sums,(ss,sr),sub=half//pieces)
    def rest(c): return pltpu.make_async_copy(down.at[c,pl.ds(half,half)],rest_hbm.at[c],rs.at[c])
    def strip(k,size): return pl.ds(pl.multiple_of(jnp.clip(k,0,size-1)*tile,tile),tile)
    def tall_load(k):
        slot=lax.rem(k,slots)
        @pl.when((k<2*first)&(lax.rem(k,2)==0))
        def _(): pltpu.make_async_copy(wgu_hbm.at[:,strip(k//2,first)],tall.at[slot],ts.at[slot]).start()
        @pl.when((k<2*first)&(lax.rem(k,2)==1))
        def _(): pltpu.make_async_copy(wgu_hbm.at[:,strip(first+k//2,2*first)],tall.at[slot],ts.at[slot]).start()
        @pl.when((k>=2*first)&(k<2*first+second))
        def _(): pltpu.make_async_copy(wd_hbm.at[:,strip(k-2*first,second)],tall.at[slot],ts.at[slot]).start()
    def tall_loaded(k):
        slot=lax.rem(k,slots)
        pltpu.make_async_copy(wd_hbm.at[:,pl.ds(0,tile)],tall.at[slot],ts.at[slot]).wait()
        return slot
    def load(k):
        slot=lax.rem(k,slots)
        late=strip((k-first)//2,second)
        @pl.when(k<first)
        def _(): pltpu.make_async_copy(wd_hbm.at[strip(k,first),:],ring.at[slot],ws.at[slot]).start()
        @pl.when((k>=first)&(lax.rem(k-first,2)==0)&(k<first+2*second))
        def _(): pltpu.make_async_copy(wgu_hbm.at[late,pl.ds(0,hidden)],ring.at[slot],ws.at[slot]).start()
        @pl.when((k>=first)&(lax.rem(k-first,2)==1)&(k<first+2*second))
        def _(): pltpu.make_async_copy(wgu_hbm.at[late,pl.ds(hidden,hidden)],ring.at[slot],ws.at[slot]).start()
    def loaded(k):
        slot=lax.rem(k,slots)
        pltpu.make_async_copy(wd_hbm.at[pl.ds(0,tile),:],ring.at[slot],ws.at[slot]).wait()
        return slot
    def own(): return pltpu.make_async_copy(grad_ref,gr.at[get.here],ls.at[0])
    def early(c): return pltpu.make_async_copy(early_hbm.at[c],gr.at[c,pl.ds(0,begun)],ls.at[1+c])
    def whole_x(): return pltpu.make_async_copy(x_hbm,x_ref,xs)
    @pl.when(s==0)
    def _():
        whole_x().start()
        for k in range(slots): tall_load(k)
        greet(get.here,count)
        get.gather_step(0,grad_ref)
        own().start()
        for c in range(count):
            @pl.when(c!=get.here)
            def _(): early(c).start()
        whole_x().wait()
    @pl.when(s==at_down-1)
    def _():
        for k in range(slots): load(k)
    hops=get.gather_steps()-1
    marks=(1,2,3,5,7) if first==4 and second==4 and hops==5 else tuple(min(k+1,at_grad) for k in range(hops))
    for k,mark in enumerate(marks):
        @pl.when(s==mark)
        def _(): get.gather_step(k+1,grad_ref)
    @pl.when(s==at_grad)
    def _():
        own().wait()
        for c in range(count):
            @pl.when(c!=get.here)
            def _(): early(c).wait()
    def finish(span,total):
        out_ref[span,:]=(res_ref[span,:]+total[...]).astype(BF)
    r=s-at_grad
    t=jnp.int32(-1)
    marks=(0,2,4,5,6,10,16) if first==4 and second==4 else tuple(range(line.far_steps()))
    for k,mark in enumerate(marks): t=jnp.where(r==mark,k,t)
    @pl.when(t>=0)
    def _(): line.far_step(t,total,finish)
    @pl.when(r==0)
    def _():
        for c in range(count): rest(c).start()
    @pl.when(s<at_down)
    def _():
        one=tall_loaded(2*s)
        two=tall_loaded(2*s+1)
        cols=strip(s,first)
        for c in range(count):
            span=slice(c*rows,(c+1)*rows)
            gate=jnp.dot(x_ref[span,:],tall[one],preferred_element_type=F32)
            up=jnp.dot(x_ref[span,:],tall[two],preferred_element_type=F32)
            sigmoid=1.0/(1.0+jnp.exp(-gate))
            active=gate*sigmoid
            product[span,cols]=(active*up).astype(BF)
            lifted[span,cols]=active.astype(BF)
            gated[span,cols]=(up*(sigmoid+active*(1.0-sigmoid))).astype(BF)
        tall_load(2*s+slots)
        tall_load(2*s+1+slots)
    @pl.when((s>=at_down)&(s<at_grad))
    def _():
        k=2*first+s-at_down
        slot=tall_loaded(k)
        sums_here=jnp.dot(product[...],tall[slot],preferred_element_type=F32).astype(BF)
        cols=strip(s-at_down,second)
        for c in range(count): down[c,:,cols]=sums_here[c*rows:(c+1)*rows]
        tall_load(k+slots)
    @pl.when((s>=at_grad)&(s<at_part))
    def _():
        k=s-at_grad
        slot=loaded(k)
        cols=strip(k,first)
        for c in range(count):
            span=slice(c*rows,(c+1)*rows)
            grads=lax.dot_general(gr[c],ring[slot],(((1,),(1,)),((),())),preferred_element_type=F32)
            gated[span,cols]=(grads*gated[span,cols].astype(F32)).astype(BF)
            lifted[span,cols]=(grads*lifted[span,cols].astype(F32)).astype(BF)
        load(k+slots)
    @pl.when((s>=at_part)&(s<at_weight))
    def _():
        k=first+2*(s-at_part)
        one=loaded(k)
        both=lax.dot_general(gated[...],ring[one],(((1,),(1,)),((),())),preferred_element_type=F32)
        load(k+slots)
        two=loaded(k+1)
        both=both+lax.dot_general(lifted[...],ring[two],(((1,),(1,)),((),())),preferred_element_type=F32)
        part_ref[...]=both.astype(BF)
        load(k+1+slots)
    last=s-at_weight
    cols=strip(last//6,second)
    kind=lax.rem(last,6)
    cut=hidden//2
    def weight(left,right):
        wide_ref[...]=lax.dot_general(left,right,(((0,),(0,)),((),())),preferred_element_type=F32).astype(BF)
    for side in (0,1):
        these=slice(side*cut,(side+1)*cut)
        @pl.when((last>=0)&(kind==side))
        def _(): weight(x_ref[:,cols],gated[:,these])
        @pl.when((last>=0)&(kind==2+side))
        def _(): weight(x_ref[:,cols],lifted[:,these])
        @pl.when((last>=0)&(kind==4+side))
        def _(): weight(gr[:,:,cols].reshape(length,tile),product[:,these])
    @pl.when(s==at_weight+6*second-1)
    def _():
        get.end_pieces()
        line.end_sums()
        for c in range(count): rest(c).wait()

def mlp(x,grad_out,residual,early,w_both,w_down,cid,spread,pieces,count):
    length,width=x.shape
    hidden=w_down.shape[0]
    rows=length//count
    tile=min(512,hidden,width)
    first,second=hidden//tile,width//tile
    steps=2*first+8*second
    assert first!=4 or second!=4 or (count-1)*pieces+1==7
    assert first+7*second>=(count-1)*pieces+1
    whole=lambda shape: pl.BlockSpec(shape,lambda s: (0,)*len(shape),pipeline_mode=pl.Buffered(1))
    hbm=pl.BlockSpec(memory_space=pl.ANY)
    sds=jax.ShapeDtypeStruct
    sem=pltpu.SemaphoreType.DMA
    at_part=2*first+second
    def wide_map(s):
        k=jnp.maximum(s-at_part-second,0)
        return (k//6,k%6)
    vmem=pltpu.VMEM
    return pl.pallas_call(functools.partial(mlp_kernel,count,pieces,tile),
        grid=(steps,),
        out_shape=(sds((length,width),BF),sds((width,3*hidden),BF),sds((rows//2,width),BF),sds((count,rows//2,width),BF)),
        in_specs=[hbm,whole((rows,width)),pl.BlockSpec((rows//2,width),lambda s: (0,0),pipeline_mode=pl.Buffered(1)),hbm,hbm,hbm],
        out_specs=(pl.BlockSpec((length,tile),lambda s: (0,jnp.clip(s-at_part,0,second-1))),
            pl.BlockSpec((tile,hidden//2),wide_map),whole((rows//2,width)),hbm),
        scratch_shapes=[vmem((length,width),BF),vmem((count,rows,width),BF),vmem((length,hidden),BF),vmem((length,hidden),BF),vmem((length,hidden),BF),
            vmem((count,rows,width),BF),vmem((4,tile,width),BF),vmem((4,width,tile),BF),vmem((count+1,rows//2,width),BF),vmem((rows//2//pieces,width),F32),
            sem((2,count,spread)),sem((2,count,spread)),sem((2,count,pieces)),sem((2,count,pieces)),sem((4,)),sem((4,)),sem((count+1,)),sem((count,)),sem],
        cost_estimate=pl.CostEstimate(flops=78_000_000_000,bytes_accessed=380_000_000,transcendentals=0),
        compiler_params=pltpu.CompilerParams(collective_id=cid,has_side_effects=True,vmem_limit_bytes=60*1024*1024,
            dimension_semantics=("arbitrary",)),
    )(x,grad_out,residual,early,w_both,w_down)


def frequencies(head_size):
    inverse = 1.0 / 500000.0 ** (jnp.arange(head_size // 2, dtype=jnp.float32) * 2.0 / head_size)
    wavelength = 2.0 * math.pi / inverse
    smooth = (8192.0 / wavelength - 1.0) / 3.0
    blended = (1.0 - smooth) * inverse / 32.0 + smooth * inverse
    return jnp.where(
        wavelength > 8192.0, inverse / 32.0, jnp.where(wavelength < 2048.0, inverse, blended)
    )


def dot(left_side, right_side, left_dim, right_dim):
    return lax.dot_general(
        left_side, right_side, (((left_dim,), (right_dim,)), ((), ())), preferred_element_type=F32
    )


def norm_kernel(count, plane, pieces, tokens_ref, gains_ref, gate_hbm, up_hbm, angles_ref, normed_hbm, gains_out, both_hbm, cosine, sine, held, normed, landed, hs, hr, ds, dr, ws, bs):
    hidden = gate_hbm.shape[1]
    sides = [
        pltpu.make_async_copy(source, both_hbm.at[:, pl.ds(k * hidden, hidden)], bs.at[k])
        for k, source in enumerate((gate_hbm, up_hbm))
    ]
    line = Line(count, pieces, tokens_ref.shape[0], held=held, held_sems=(hs, hr))
    greet(line.here, count, plane)
    me = lax.axis_index(DP)
    begin, end = swap(DP, plane, lambda p: gains_ref, landed, ds, dr)
    for u in range(pieces):
        line.send_own(u, tokens_ref.at[line.span(u), :])
    begin()
    for side in sides:
        side.start()
    landed[me] = gains_ref[...]
    end()
    piece = gains_ref.shape[1]
    for p in range(plane):
        gains_out[:, p * piece : (p + 1) * piece] = landed[p]

    def give(c, u):
        return pltpu.make_async_copy(normed.at[c, line.span(u)], normed_hbm.at[c, line.span(u)], ws.at[c, u])

    def norm(rows, c, u):
        stream = rows.astype(F32)
        scale = lax.rsqrt(jnp.mean(stream * stream, -1, keepdims=True) + EPSILON)
        normed[c, line.span(u)] = (stream * scale * gains_out[0:1, :]).astype(BF)
        give(c, u).start()

    def step(t, _):
        line.pass_pieces(t, lambda c, u: norm(held[c, line.span(u)], c, u))

        @pl.when(t == 1)
        def _():
            cosine[...] = jnp.cos(angles_ref[...])
            sine[...] = jnp.sin(angles_ref[...])

        @pl.when(t < pieces)
        def _():
            u = jnp.clip(t, 0, pieces - 1)
            norm(tokens_ref[line.span(u), :], line.here, u)

        return 0

    lax.fori_loop(0, pieces + count - 1, step, 0)
    line.end_pieces()
    for side in sides:
        side.wait()
    for c in range(count):
        for u in range(pieces):
            give(c, u).wait()


def norm_and_gather(tokens, gains, w_gate, w_up, angles, cid, pieces, count, plane):
    rows, width = tokens.shape
    vm = pl.BlockSpec(memory_space=pltpu.VMEM)
    sem = pltpu.SemaphoreType.DMA
    hbm = pl.BlockSpec(memory_space=pl.ANY)
    sds = jax.ShapeDtypeStruct
    normed, *rest = pl.pallas_call(
        functools.partial(norm_kernel, count, plane, pieces),
        out_shape=(
            sds((count, rows, width), BF),
            sds((8, width), F32),
            sds((w_gate.shape[0], 2 * w_gate.shape[1]), BF),
            sds(angles.shape, F32),
            sds(angles.shape, F32),
        ),
        in_specs=[vm, vm, hbm, hbm, vm],
        out_specs=(hbm, vm, hbm, vm, vm),
        scratch_shapes=[
            pltpu.VMEM((count, rows, width), BF),
            pltpu.VMEM((count, rows, width), BF),
            pltpu.VMEM((plane, 8, width // plane), F32),
            sem((2, count, pieces)),
            sem((2, count, pieces)),
            sem((plane,)),
            sem((plane,)),
            sem((count, pieces)),
            sem((2,)),
        ],
        cost_estimate=pl.CostEstimate(flops=0, bytes_accessed=270_000_000, transcendentals=0),
        compiler_params=pltpu.CompilerParams(
            collective_id=cid, has_side_effects=True, vmem_limit_bytes=58 * 1024 * 1024
        ),
    )(tokens, gains, w_gate, w_up, angles)
    return normed.reshape(count * rows, width), *rest


def wide_results_kernel(gate_in, up_in, down_in, tokens_in, block_in, sums_ref, gains_ref, gate, up, down, tokens, block, terms):
    tokens[...] = tokens_in[...]
    block[...] = block_in[...]
    terms[0:1, :] = jnp.sum(sums_ref[0:8, :], 0, keepdims=True) / gains_ref[0:1, :]
    terms[1:2, :] = jnp.sum(sums_ref[8:16, :], 0, keepdims=True) / gains_ref[1:2, :]
    gate[...] = gate_in[...].astype(F32)
    up[...] = up_in[...].astype(F32)
    down[...] = down_in[...].astype(F32).T


def wide_results(wide, grad_tokens, block_out, sums, gains, hidden):
    shard = wide.shape[0]
    tile = min(512, hidden)
    steps = hidden // tile
    sds = jax.ShapeDtypeStruct
    still = lambda shape: pl.BlockSpec(shape, lambda s: (0, 0))
    strip = pl.BlockSpec((grad_tokens.shape[0], grad_tokens.shape[1] // steps), lambda s: (0, s))
    return pl.pallas_call(
        wide_results_kernel,
        grid=(steps,),
        out_shape=(
            sds((shard, hidden), F32),
            sds((shard, hidden), F32),
            sds((hidden, shard), F32),
            sds(grad_tokens.shape, F32),
            sds(block_out.shape, BF),
            sds((2, shard), F32),
        ),
        in_specs=[pl.BlockSpec((shard, tile), lambda s, k=k: (0, k * steps + s)) for k in range(3)]
        + [strip, strip, still(sums.shape), still(gains.shape)],
        out_specs=(
            pl.BlockSpec((shard, tile), lambda s: (0, s)),
            pl.BlockSpec((shard, tile), lambda s: (0, s)),
            pl.BlockSpec((tile, shard), lambda s: (s, 0)),
            strip,
            strip,
            still((2, shard)),
        ),
        compiler_params=pltpu.CompilerParams(vmem_limit_bytes=60 * 1024 * 1024),
    )(wide, wide, wide, grad_tokens, block_out, sums, gains)


def mix_results_kernel(mix_ref, terms_ref, query, key, value, out, first, second):
    edge = query.shape[1]
    query[...] = mix_ref[:, :edge].astype(F32)
    key[...] = mix_ref[:, edge : edge + key.shape[1]].astype(F32)
    edge += key.shape[1]
    value[...] = mix_ref[:, edge : edge + value.shape[1]].astype(F32)
    edge += value.shape[1]
    out[...] = mix_ref[:, edge:].astype(F32).T
    first[...] = terms_ref[0:1, :]
    second[...] = terms_ref[1:2, :]


def mix_results(mix, terms, deep, narrow):
    shard = mix.shape[0]
    sds = jax.ShapeDtypeStruct
    vm = pl.BlockSpec(memory_space=pltpu.VMEM)
    return pl.pallas_call(
        mix_results_kernel,
        out_shape=(
            sds((shard, deep), F32),
            sds((shard, narrow), F32),
            sds((shard, narrow), F32),
            sds((deep, shard), F32),
            sds((1, shard), F32),
            sds((1, shard), F32),
        ),
        in_specs=[vm, vm],
        out_specs=(vm,) * 6,
        compiler_params=pltpu.CompilerParams(vmem_limit_bytes=60 * 1024 * 1024),
    )(mix, terms)


def body(
    count,
    plane,
    tokens,
    segments,
    positions,
    attn_gain,
    w_query,
    w_key,
    w_value,
    w_out,
    mlp_gain,
    w_gate,
    w_up,
    w_down,
    grad_out,
):
    rows, width = tokens.shape
    heads = w_query.shape[1] // HD
    groups = w_key.shape[1] // HD
    after = lax.optimization_barrier
    mix = lax.all_gather(jnp.concatenate([w_query, w_key, w_value], 1), DP, axis=0, tiled=True)
    full_out = lax.all_gather(w_out, DP, axis=1, tiled=True)
    full_down = lax.all_gather(w_down, DP, axis=1, tiled=True)
    own_gains = jnp.concatenate([jnp.stack([attn_gain, mlp_gain]).astype(F32), jnp.zeros((6, attn_gain.shape[0]), F32)])

    angles = frequencies(HD)[:, None] * positions.astype(F32)[None, :]
    normed_one, gains, both, cosine, sine = norm_and_gather(tokens, own_gains, w_gate, w_up, angles, 1, 4, count, plane)
    full_both = lax.all_gather(both, DP, axis=0, tiled=True)

    mixed, lse, q, kt, k, v, residual, early, normed_two = attend(
        mix, normed_one, cosine, sine, segments, full_out, grad_out, tokens, gains, heads, groups, 6, rows * 5 // 8, 5, 16, count
    )
    normed_two = normed_two.reshape(count * rows, width)
    part, grad_wide, block_early, down = mlp(normed_two, grad_out, residual, early, full_both, full_down, 5, 3, 2, count)
    grad_wide = lax.psum_scatter(grad_wide, DP, scatter_dimension=0, tiled=True)
    grad_residual, terms_two, part, grad_mix, block_out = attend_back(
        part, normed_two, grad_out, gains, full_out, q, kt, k, v, lse, cosine, sine, segments, down, residual, block_early,
        mixed, normed_one, mix, heads, groups, 7, 2, 16, count,
    )
    grad_mix = lax.psum_scatter(grad_mix, DP, scatter_dimension=0, tiled=True)
    grad_tokens, sums = last_sums(part, normed_one, tokens, grad_residual, gains, terms_two, 4, 4, count, plane)
    grad_gate, grad_up, grad_down, grad_tokens, block_out, terms = wide_results(
        grad_wide, grad_tokens, block_out, sums, own_gains, full_down.shape[0]
    )
    grad_query, grad_key, grad_value, grad_out_proj, grad_attn_gain, grad_mlp_gain = mix_results(
        grad_mix, terms, heads * HD, groups * HD
    )
    return (
        block_out,
        grad_tokens,
        grad_attn_gain.reshape(-1),
        grad_query,
        grad_key,
        grad_value,
        grad_out_proj,
        grad_mlp_gain.reshape(-1),
        grad_gate,
        grad_up,
        grad_down,
    )


def solution(mesh):
    placed = (
        P(("dp", "tensor"), None),
        P("dp"),
        P("dp"),
        P("dp"),
        P("dp", "tensor"),
        P("dp", "tensor"),
        P("dp", "tensor"),
        P("tensor", "dp"),
        P("dp"),
        P("dp", "tensor"),
        P("dp", "tensor"),
        P("tensor", "dp"),
        P(("dp", "tensor"), None),
    )
    return jax.shard_map(
        functools.partial(body, mesh.shape["tensor"], mesh.shape["dp"]),
        mesh=mesh,
        in_specs=placed,
        out_specs=(
            P(("dp", "tensor"), None),
            P(("dp", "tensor"), None),
            P("dp"),
            P("dp", "tensor"),
            P("dp", "tensor"),
            P("dp", "tensor"),
            P("tensor", "dp"),
            P("dp"),
            P("dp", "tensor"),
            P("dp", "tensor"),
            P("tensor", "dp"),
        ),
        check_vma=False,
    )
```

profile of v0, /device:TPU:0, one launch (start us, length us, event | category | flops | bytes accessed | tf_op | source)
XLA Modules:
  0.0 596.7 jit_solution(12184322478488311708)
XLA Ops:
  7.2 0.0 all-gather.7.cloned.1.call-start
  7.2 0.7 all-gather.7.cloned.1.call-update
  7.9 0.0 all-gather.5.cloned.1.call-start
  8.0 1.8 pad_maximum_fusion
  9.8 0.0 all-gather.5.cloned.1.call-update
  9.8 0.0 all-gather.11.cloned.1.call-start
  9.8 0.7 all-gather.11.cloned.1.call-update
  10.5 0.0 all-gather.9.cloned.1.call-start
  10.6 0.7 stack.9
  11.2 0.7 stack.10
  11.9 0.7 convert_element_type.4
  12.6 0.6 fusion.3.gains_ref
  13.2 0.7 broadcast_multiply_fusion.angles_ref
  13.9 77.6 %shard_map.212 = (bf16[4,256,2048]{2,1,0:T(8,128)(2,1)}, f32[8,2048]{1,0:T(8,128)}, bf16[256,4096]{1,0:T(8,128)(2,1)}, f32[32,1024]{1,0:T(8,128)}, f32[32,1024]{1,0:T(8,128)}) custom-call(bf16[256,2048]{1,0:T(8,128)(2,1)} %tokens_hbm.3, f32[8,256]{1,0:T(8,128)} %fusion.3.gains_ref, bf16[256,2048]{1,0:T(8,128)(2,1)} %gate_hbm.1, bf16[256,2048]{1,0:T(8,128)(2,1)} %up_hbm.1, ...), custom_call_target="tpu_custom_call" | custom-call | bytes 270000000 | tf_op jit(solution)/shard_map/pallas_call | solution.py:804
  91.5 0.0 all-gather.9.cloned.1.call-update
  91.6 0.0 reduce-scatter.3.cloned.1.call-start
  91.6 0.0 all-gather.7.cloned.1.call-done.wo_hbm
  91.6 0.0 all-gather.5.cloned.1.call-done.mix_hbm
  91.7 148.5 %shard_map.213 = (bf16[512,1024]{1,0:T(8,128)(2,1)}, f32[8,1,1024]{2,1,0:T(1,128)}, bf16[512,1024]{1,0:T(8,128)(2,1)}, bf16[128,1024]{1,0:T(8,128)(2,1)}, bf16[2...) custom-call(bf16[2048,768]{1,0:T(8,128)(2,1)} %all-gather.5.cloned.1, ...), custom_call_target="tpu_custom_call" | custom-call | flops 30000001024 | bytes 500000000 | tf_op jit(solution)/shard_map/pallas_call | solution.py:140
  240.1 0.0 all-gather.11.cloned.1.call-done.wd_hbm
  240.2 0.0 all-gather.9.cloned.1.call-done.wgu_hbm
  240.2 108.2 %shard_map.214 = (bf16[1024,2048]{1,0:T(8,128)(2,1)}, bf16[2048,6144]{1,0:T(8,128)(2,1)}, bf16[128,2048]{1,0:T(8,128)(2,1)}, bf16[4,128,2048]{2,1,0:T(8,128)(2,1)}) custom-call(bf16[1024,2048]{1,0:T(8,128)(2,1)} %bitcast.11, bf16[256,2048]{1,0:T(8,128)(2,1)} %go_ref.1, f32[256,2048]{1,0:T(8,128)} %get-tuple-element.53.res_ref, ...), custom_call_target="tpu_custom_call" | custom-call | flops 77999996928 | bytes 380000000 | tf_op jit(solution)/shard_map/pallas_call | solution.py:713
  348.4 0.0 reduce-scatter.3.cloned.1.call-update
  348.4 0.0 reduce-scatter.5.cloned.1.call-start
  348.5 159.3 %shard_map.215 = (f32[256,2048]{1,0:T(8,128)}, f32[8,2048]{1,0:T(8,128)}, bf16[4,256,2048]{2,1,0:T(8,128)(2,1)}, bf16[2048,1280]{1,0:T(8,128)(2,1)}, bf16[256,2048]{1,0:T(8,128)(2,1)}) custom-call(bf16[4,256,2048]{2,1,0:T(8,128)(2,1)} %bitcast.12, bf16[4,256,2048]{2,1,0:T(8,128)(2,1)} %get-tuple-element.52.two_hbm, bf16[256,2048]{1,0:T(8,128)(2,1)} %go_ref.1, ...), custom_call_target="tpu_custom_call" | custom-call | flops 60000002048 | bytes 550000000 | tf_op jit(solution)/shard_map/pallas_call | solution.py:293
  507.8 0.0 reduce-scatter.5.cloned.1.call-update
  507.9 72.6 %shard_map.216 = (f32[256,2048]{1,0:T(8,128)}, f32[16,256]{1,0:T(8,128)}) custom-call(bf16[4,256,2048]{2,1,0:T(8,128)(2,1)} %get-tuple-element.66.part_hbm, bf16[4,256,2048]{2,1,0:T(8,128)(2,1)} %get-tuple-element.48.normed_hbm.other_hbm, bf16[256,2048]{1,0:T(8,128)(2,1)} %tokens_hbm.3, f32[256,2048]{1,0:T(8,128)} %get-tuple-element.67.grads_hbm, ...), custom_call_target="tpu_custom_call" | custom-call | bytes 270000000 | tf_op jit(solution)/shard_map/pallas_call | solution.py:540
  580.5 0.0 reduce-scatter.3.cloned.1.call-done.gate_in.up_in.down_in
  580.5 6.8 %shard_map.217 = (f32[256,2048]{1,0:T(8,128)}, f32[256,2048]{1,0:T(8,128)}, f32[2048,256]{1,0:T(8,128)}, f32[256,2048]{1,0:T(8,128)}, bf16[256,2048]{1,0:T(8,128)(2,1)}, /*index=5*/f32[2,256]{1,0:T(2,128)}) custom-call(bf16[256,6144]{1,0:T(8,128)(2,1)} %reduce-scatter.3.cloned.1.call-done.gate_in.up_in.down_in, ...), custom_call_target="tpu_custom_call" | custom-call | tf_op jit(solution)/shard_map/pallas_call | solution.py:851
  587.3 0.0 reduce-scatter.5.cloned.1.call-done.mix_ref
  587.4 2.2 shard_map.218
  (1 shorter events, 0.0 us)
Async XLA Ops:
  7.2 84.4 %all-gather.7.cloned.1.call-start = ((), (), s32[]{:S(2)}) async-start(), calls=%async_computation.3 | async-start | bytes 2359296 | tf_op jit(solution)/shard_map/all_gather | solution.py:930
  7.9 83.7 %all-gather.5.cloned.1.call-start = ((), (), s32[]{:S(2)}) async-start(), calls=%async_computation.2 | async-start | bytes 3538944 | tf_op jit(solution)/shard_map/all_gather | solution.py:929
  9.8 230.4 %all-gather.11.cloned.1.call-start = ((), (), s32[]{:S(2)}) async-start(), calls=%async_computation.5 | async-start | bytes 9437184 | tf_op jit(solution)/shard_map/all_gather | solution.py:931
  10.5 229.6 %all-gather.9.cloned.1.call-start = ((), (), s32[]{:S(2)}) async-start(), calls=%async_computation.4 | async-start | bytes 18874368 | tf_op jit(solution)/shard_map/all_gather | solution.py:936
  91.6 488.9 %reduce-scatter.3.cloned.1.call-start = ((), (), s32[]{:S(2)}) async-start(), calls=%async_computation.6 | async-start | bytes 28311552 | tf_op jit(solution)/shard_map/reduce_scatter | solution.py:943
  348.4 238.9 %reduce-scatter.5.cloned.1.call-start = ((), (), s32[]{:S(2)}) async-start(), calls=%async_computation.7 | async-start | bytes 5898240 | tf_op jit(solution)/shard_map/reduce_scatter | solution.py:948
Sparse Core Ops, SparseCore 0:
  9.9 30.8 all-gather.6
  43.3 32.3 all-gather.4
  77.5 55.9 all-gather.10
  135.3 89.8 all-gather.8
  348.6 160.6 reduce-scatter.2
  512.4 56.5 reduce-scatter.4
where the time goes:
time: 605 us; the launch traced here: 597 us
  Pallas kernels  575 us (95%)
  between operations  14.4 us (2%)
    pallas_call x1, Pallas kernels, attend_back(): pl.pallas_call(functools.partial(attend_back_kernel, heads, groups, block...  159 us
    pallas_call x1, Pallas kernels, attend(): pl.pallas_call(functools.partial(attend_kernel, heads, groups, block, cou...  148 us
    pallas_call x1, Pallas kernels, mlp(): pl.pallas_call(functools.partial(mlp_kernel, count, pieces, tile), grid=(...  108 us
    pallas_call x1, Pallas kernels, norm_and_gather(): pl.pallas_call(functools.partial(norm_kernel, count, plane, pieces), out_...  77.6 us
    pallas_call x1, Pallas kernels, last_sums(): pl.pallas_call(functools.partial(last_kernel, n, plane, pieces), out_shap...  72.6 us
  transfers between devices with their start and end apart: 6, of which 0 were waited for; matrix products, arithmetic and copies ran while one was open for 1% of the time, Pallas kernels for 78%

commit v1 on v0

--- a/solution.py
+++ b/solution.py
@@ -19,19 +19,26 @@
     first, second = values[:half], values[half:]
     return jnp.concatenate([first*cosine - sign*second*sine, second*cosine + sign*first*sine],0)
 
-def column(row_ref):
-    return jnp.broadcast_to(row_ref[...].astype(F32),(8,row_ref.shape[1])).T[:,0:1].astype(jnp.int32)
-
-def block_bias(segs_col, segs_row, start, block):
-    keys=start+block
-    key_places=lax.broadcasted_iota(jnp.int32,(keys,block),0)
-    query_places=start+lax.broadcasted_iota(jnp.int32,(keys,block),1)
-    allowed=(key_places<=query_places)&(segs_col[0:keys,:]==segs_row[0:1,start:start+block])
-    return jnp.where(allowed,0.0,MASKED).astype(F32)
+AUG=80
+
+def thirds(x):
+    one=x.astype(BF)
+    rest=x-one.astype(F32)
+    two=rest.astype(BF)
+    three=(rest-two.astype(F32)).astype(BF)
+    return [part.astype(F32) for part in (one,two,three)]
+
+def tail_rows(rows,width):
+    return jnp.concatenate(rows+[jnp.zeros((AUG-HD-len(rows),width),F32)],0)
+
+def triangle(block):
+    keys=lax.broadcasted_iota(jnp.int32,(block,block),0)
+    queries=lax.broadcasted_iota(jnp.int32,(block,block),1)
+    return jnp.where(keys<=queries,0.0,MASKED).astype(F32)
 
 def attend_kernel(heads, groups, block, count, pieces, fine, mix_hbm, normed_hbm, cos_ref, sin_ref, segr_ref, wo_hbm, grad_ref, tokens_hbm, gain_ref,
-                  mixed_ref, lse_ref, q_ref, kt_ref, k_ref, v_ref, residual_ref, rows_hbm, whole_hbm,
-                  mix_ref, normed_ref, lin_ref, bias_ref, vt_ref, wo_ref, tokens_ref, part_ref, held, hs, hr, sums, total, ss, sr, moved, ms, mr, cs):
+                  mixed_ref, q_ref, kt_ref, k_ref, v_ref, residual_ref, rows_hbm, whole_hbm,
+                  mix_ref, normed_ref, lin_ref, tri_ref, vt_ref, wo_ref, tokens_ref, part_ref, held, hs, hr, sums, total, ss, sr, moved, ms, mr, cs):
     length=normed_ref.shape[0]
     per=heads//groups
     rows=grad_ref.shape[0]
@@ -59,40 +66,45 @@
             line.gather_step(done,grad_ref)
     tick()
     cosine, sine = cos_ref[...], sin_ref[...]
+    segs=segr_ref[...]
+    apart=[jnp.where(segs==s,MASKED,0.0).astype(F32) for s in range(3)]
+    others=[jnp.where(segs==s,0.0,1.0).astype(F32) for s in range(3)]
+    ones=jnp.ones((1,length),F32)
+    plain=tail_rows(apart,length).astype(BF)
     def rope(h,_):
         rows=pl.ds(pl.multiple_of(h*HD,HD),HD)
-        q_ref[rows,:]=(turn_t(lin_ref[rows,:],cosine,sine,1.0).astype(BF)*jnp.asarray(0.125,BF))
+        q_ref[h,0:HD,:]=(turn_t(lin_ref[rows,:],cosine,sine,1.0).astype(BF)*jnp.asarray(0.125,BF))
+        q_ref[h,HD:,:]=plain
         return 0
     lax.fori_loop(0,heads,rope,0)
-    turned=[turn_t(lin_ref[(heads+g)*HD:(heads+g+1)*HD,:],cosine,sine,1.0) for g in range(groups)]
-    keys_t=jnp.concatenate(turned,0)
-    kt_ref[...]=keys_t.astype(BF)
-    vals_t=lin_ref[(heads+groups)*HD:(heads+2*groups)*HD,:]
-    vt_ref[...]=vals_t.astype(BF)
-    keys_n=keys_t.T.astype(BF)
-    vals_n=vals_t.T.astype(BF)
+    beside=tail_rows(others+[ones]*3,length)
+    below=tail_rows([ones]*3,length)
     for g in range(groups):
-        k_ref[g]=keys_n[:,g*HD:(g+1)*HD]
-        v_ref[g]=vals_n[:,g*HD:(g+1)*HD]
-    segs_col=column(segr_ref)
+        keys_t=turn_t(lin_ref[(heads+g)*HD:(heads+g+1)*HD,:],cosine,sine,1.0)
+        kt_ref[g*HD:(g+1)*HD,:]=keys_t.astype(BF)
+        k_ref[g]=jnp.concatenate([keys_t,beside],0).T.astype(BF)
+        vals_t=jnp.concatenate([lin_ref[(heads+groups+g)*HD:(heads+groups+g+1)*HD,:],below],0)
+        vt_ref[g]=vals_t.astype(BF)
+        v_ref[g]=vals_t.T.astype(BF)
+    tri_ref[...]=triangle(block)
     for start in range(0,length,block):
-        keys=start+block
+        cols=slice(start,start+block)
         if start in (block,3*block): tick()
-        bias_ref[0:keys,:]=block_bias(segs_col,segr_ref,start,block)
         def head(h,_):
             g=h//per
             rows=pl.ds(pl.multiple_of(h*HD,HD),HD)
-            grows=pl.ds(pl.multiple_of(g*HD,HD),HD)
-            scores=jnp.dot(k_ref[g,0:keys,:],q_ref[rows,start:start+block],preferred_element_type=F32)
-            scores=scores+bias_ref[0:keys,:]
-            top=jnp.max(scores,0,keepdims=True)
-            weights=jnp.exp(scores-top)
-            total=jnp.sum(weights,0,keepdims=True)
-            out=jnp.dot(vt_ref[grows,0:keys],weights.astype(BF),preferred_element_type=F32)
-            mixed_ref[rows,start:start+block]=(out/total).astype(BF)
-            lse_ref[h,:,start:start+block]=top+jnp.log(total)
+            query=q_ref[h,:,cols]
+            parts=[jnp.dot(k_ref[g,c:c+block,:],query,preferred_element_type=F32) for c in range(0,start+block,block)]
+            parts[-1]=parts[-1]+tri_ref[...]
+            top=functools.reduce(jnp.maximum,[jnp.max(part,0,keepdims=True) for part in parts])
+            out=functools.reduce(jnp.add,[jnp.dot(vt_ref[g,:,k*block:(k+1)*block],jnp.exp(part-top).astype(BF),preferred_element_type=F32)
+                for k,part in enumerate(parts)])
+            total=out[HD:HD+1]
+            mixed_ref[rows,cols]=(out[:HD]/total).astype(BF)
+            logs=thirds(top+jnp.log(total))
+            q_ref[h,HD:,cols]=tail_rows([row[:,cols] for row in apart]+[-x for x in logs],block).astype(BF)
             return 0
-        lax.fori_loop(0,heads,head,0)
+        lax.fori_loop(0,heads,head,0,unroll=2)
     width=wo_ref.shape[1]
     wide=min(512,width)
     weights.wait()
@@ -138,11 +150,11 @@
     sem=pltpu.SemaphoreType.DMA
     vmem=pltpu.VMEM
     return pl.pallas_call(functools.partial(attend_kernel,heads,groups,block,count,pieces,fine),
-        out_shape=(sds((heads*HD,length),BF),sds((heads,1,length),F32),sds((heads*HD,length),BF),
-            sds((groups*HD,length),BF),sds((groups,length,HD),BF),sds((groups,length,HD),BF),
+        out_shape=(sds((heads*HD,length),BF),sds((heads,AUG,length),BF),
+            sds((groups*HD,length),BF),sds((groups,length,AUG),BF),sds((groups,length,AUG),BF),
             sds((rows,width),F32),sds((count,early,width),BF),sds((count,rows,width),BF)),
-        in_specs=[hbm,hbm]+[vm]*3+[hbm,vm,hbm,vm],out_specs=(vm,)*7+(hbm,hbm),
-        scratch_shapes=[vmem(mix.shape,BF),vmem(normed.shape,BF),vmem((mix.shape[1],length),F32),vmem((length,block),F32),vmem((groups*HD,length),BF),vmem(w_out.shape,BF),
+        in_specs=[hbm,hbm]+[vm]*3+[hbm,vm,hbm,vm],out_specs=(vm,)*6+(hbm,hbm),
+        scratch_shapes=[vmem(mix.shape,BF),vmem(normed.shape,BF),vmem((mix.shape[1],length),F32),vmem((block,block),F32),vmem((groups,AUG,length),BF),vmem(w_out.shape,BF),
             vmem(tokens.shape,BF),vmem((count,rows,width),BF),vmem((count,early,width),BF),sem((2,count,pieces)),sem((2,count,pieces)),
             vmem((count+1,rows,width),BF),vmem((rows//fine,width),F32),sem((2,count,fine)),sem((2,count,fine)),
             vmem((count,rows,width),BF),sem((2,count,fine)),sem((2,count,fine)),sem((6,))],
@@ -150,12 +162,12 @@
         compiler_params=pltpu.CompilerParams(collective_id=cid,has_side_effects=True,vmem_limit_bytes=58*1024*1024),
     )(mix,normed,cosine,sine,segments.reshape(1,length),w_out,grad_out,tokens,gain)
 
-def attend_back_kernel(heads, groups, block, count, pieces, fine, grads_hbm, two_hbm, go_ref, gain_ref, wo_hbm, q_ref, kt_ref, k_ref, v_ref, lse_ref, cos_ref, sin_ref, segr_ref,
+def attend_back_kernel(heads, groups, block, count, pieces, fine, grads_hbm, two_hbm, go_ref, gain_ref, wo_hbm, q_ref, kt_ref, k_ref, v_ref, cos_ref, sin_ref,
                   down_ref, res_ref, early_ref, mixed_hbm, normed_hbm, mix_hbm,
                   gres_ref, acc, part_hbm, grad_hbm, out_ref,
                   part_ref, normed_ref, low_ref, wide_sums, wide_total, ws, wr, hs, hr,
-                  wo_ref, mixed_ref, mix_ref, turn_ref, gm_ref, bias_ref, qn_ref, gn_ref, dq_ref, dk_ref, dv_ref, sums, total, ss, sr, grad_ref, cs, gs_sem):
-    length=q_ref.shape[1]
+                  wo_ref, mixed_ref, mix_ref, turn_ref, gm_ref, tri_ref, qn_ref, gn_ref, dq_ref, dk_ref, dv_ref, sums, total, ss, sr, grad_ref, cs, gs_sem):
+    length=q_ref.shape[2]
     per=heads//groups
     width=wo_ref.shape[1]
     rows=res_ref.shape[0]
@@ -185,8 +197,17 @@
         out_ref[places,:]=(res_ref[places,:]+total[...]).astype(BF)
     steps=sweep.sweep_steps()
     begun=2
+    dk_ref[...]=jnp.zeros_like(dk_ref)
+    dv_ref[...]=jnp.zeros_like(dv_ref)
+    tri_ref[...]=triangle(block)
+    def flip_query(p):
+        qn=jnp.concatenate([q_ref[2*p,0:HD,:],q_ref[2*p+1,0:HD,:]],0).astype(F32).T.astype(BF)
+        qn_ref[2*p]=qn[:,:HD]
+        qn_ref[2*p+1]=qn[:,HD:]
     def step(t,_):
         sweep.sweep(t,wide_total,turn)
+        @pl.when((t>=8)&(t<8+heads//2))
+        def _(): flip_query(jnp.clip(t-8,0,heads//2-1))
         @pl.when(t==2)
         def _(): second.wait()
         @pl.when((t>=2)&(t<count+2))
@@ -209,46 +230,47 @@
     cosine, sine = cos_ref[...], sin_ref[...]
     deep=heads*HD
     cut=256 if deep%256==0 else deep
+    late[0].wait()
     for c in range(0,deep,cut):
-        gm_ref[c:c+cut,:]=lax.dot_general(wo_ref[c:c+cut,:],whole(),(((1,),(1,)),((),())),preferred_element_type=F32).astype(BF)
+        product=lax.dot_general(wo_ref[c:c+cut,:],whole(),(((1,),(1,)),((),())),preferred_element_type=F32).astype(BF)
+        for h in range(c//HD,(c+cut)//HD):
+            grads=product[h*HD-c:(h+1)*HD-c]
+            gm_ref[h,0:HD,:]=grads
+            centre=jnp.sum(grads.astype(F32)*mixed_ref[h*HD:(h+1)*HD,:].astype(F32),0,keepdims=True)
+            gm_ref[h,HD:,:]=tail_rows([-x for x in thirds(centre)],length).astype(BF)
     def flip(p,_):
-        rows=pl.ds(pl.multiple_of(p*2*HD,2*HD),2*HD)
-        qn=q_ref[rows,:].astype(F32).T.astype(BF)
-        gn=gm_ref[rows,:].astype(F32).T.astype(BF)
-        qn_ref[2*p]=qn[:,:HD]
-        qn_ref[2*p+1]=qn[:,HD:]
+        gn=jnp.concatenate([gm_ref[2*p,0:HD,:],gm_ref[2*p+1,0:HD,:]],0).astype(F32).T.astype(BF)
         gn_ref[2*p]=gn[:,:HD]
         gn_ref[2*p+1]=gn[:,HD:]
         return 0
     lax.fori_loop(0,heads//2,flip,0)
-    dk_ref[...]=jnp.zeros_like(dk_ref)
-    dv_ref[...]=jnp.zeros_like(dv_ref)
     lines=(heads+2*groups)*HD
     strip=min(512,width)
-    late[0].wait()
     tick()
     for c in range(0,width,strip):
         grad_ref[c:c+strip,lines:]=lax.dot_general(low_ref[:,:,c:c+strip].reshape(length,strip),mixed_ref[...],(((0,),(1,)),((),())),preferred_element_type=F32).astype(BF)
-    segs_col=column(segr_ref)
     for start in range(0,length,block):
-        keys=start+block
         cols=slice(start,start+block)
-        bias_ref[0:keys,:]=block_bias(segs_col,segr_ref,start,block)
+        spans=[slice(start,start+block)]+([slice(0,start)] if start else [])
         def head(h,_):
             g=h//per
             rows=pl.ds(pl.multiple_of(h*HD,HD),HD)
             grows=pl.ds(pl.multiple_of(g*HD,HD),HD)
-            scores=jnp.dot(k_ref[g,0:keys,:],q_ref[rows,cols],preferred_element_type=F32)
-            probs=jnp.exp(scores+bias_ref[0:keys,:]-lse_ref[h,:,cols])
-            dv_ref[g,0:keys,:]+=jnp.dot(probs.astype(BF),gn_ref[h,cols,:],preferred_element_type=F32)
-            gp=jnp.dot(v_ref[g,0:keys,:],gm_ref[rows,cols],preferred_element_type=F32)
-            weighted=probs*gp
-            centre=jnp.sum(weighted,0,keepdims=True)
-            gs=(weighted-probs*centre).astype(BF)
-            dk_ref[g,0:keys,:]+=jnp.dot(gs,qn_ref[h,cols,:],preferred_element_type=F32)
-            dq_ref[rows,cols]=0.125*jnp.dot(kt_ref[grows,0:keys],gs,preferred_element_type=F32)
+            query,grads=q_ref[h,:,cols],gm_ref[h,:,cols]
+            query_n,grads_n=qn_ref[h,cols,:],gn_ref[h,cols,:]
+            total_q=None
+            for k,span in enumerate(spans):
+                scores=jnp.dot(k_ref[g,span,:],query,preferred_element_type=F32)
+                if k==0: scores=scores+tri_ref[...]
+                probs=jnp.exp(scores)
+                dv_ref[g,span,:]+=jnp.dot(probs.astype(BF),grads_n,preferred_element_type=F32)
+                gs=(probs*jnp.dot(v_ref[g,span,:],grads,preferred_element_type=F32)).astype(BF)
+                dk_ref[g,span,:]+=jnp.dot(gs,query_n,preferred_element_type=F32)
+                one=jnp.dot(kt_ref[grows,span],gs,preferred_element_type=F32)
+                total_q=one if total_q is None else total_q+one
+            dq_ref[rows,cols]=0.125*total_q
             return 0
-        lax.fori_loop(0,heads,head,0)
+        lax.fori_loop(0,heads,head,0,unroll=2)
         if start>0: tick()
     def back(h,_):
         rows=pl.ds(pl.multiple_of(h*HD,HD),HD)
@@ -279,7 +301,7 @@
     for k,c in enumerate(range(0,width,strip)):
         pltpu.make_async_copy(grad_ref.at[c:c+strip],grad_hbm.at[c:c+strip],gs_sem.at[k]).wait()
 
-def attend_back(grads,two,grad_out,gain,w_out,q,kt,k,v,lse,cosine,sine,segments,down,residual,early,mixed,normed,mix,heads,groups,cid,pieces,fine,count):
+def attend_back(grads,two,grad_out,gain,w_out,q,kt,k,v,cosine,sine,down,residual,early,mixed,normed,mix,heads,groups,cid,pieces,fine,count):
     rows,width=residual.shape
     length=rows*count
     lines=mix.shape[1]
@@ -292,17 +314,17 @@
     cut=lambda x: x.reshape(count,rows,width)
     return pl.pallas_call(functools.partial(attend_back_kernel,heads,groups,block,count,pieces,fine),
         out_shape=(sds((rows,width),F32),sds((8,width),F32),sds((count,rows,width),BF),sds((width,lines+heads*HD),BF),sds((rows,width),BF)),
-        in_specs=[hbm,hbm,vm,vm,hbm]+[vm]*11+[hbm]*3,out_specs=(vm,vm,hbm,hbm,vm),
+        in_specs=[hbm,hbm,vm,vm,hbm]+[vm]*9+[hbm]*3,out_specs=(vm,vm,hbm,hbm,vm),
         scratch_shapes=[vmem((count,rows,width),BF),vmem((count,rows,width),BF),vmem((count,rows,width),BF),vmem((count+1,rows,width),BF),
             vmem((rows//fine,width),F32),sem((2,count,fine)),sem((2,count,fine)),sem((2,count,fine)),sem((2,count,fine)),
-            vmem(w_out.shape,BF),vmem(mixed.shape,BF),vmem(mix.shape,BF),vmem((lines,length),BF),vmem((heads*HD,length),BF),
-            vmem((length,block),F32),vmem((heads,length,HD),BF),vmem((heads,length,HD),BF),
+            vmem(w_out.shape,BF),vmem(mixed.shape,BF),vmem(mix.shape,BF),vmem((lines,length),BF),vmem((heads,AUG,length),BF),
+            vmem((block,block),F32),vmem((heads,length,HD),BF),vmem((heads,length,HD),BF),
             vmem((heads*HD,length),F32),vmem((groups,length,HD),F32),vmem((groups,length,HD),F32),
             vmem((count+1,rows//2,width),BF),vmem((rows//2//pieces,width),F32),sem((2,count,pieces)),sem((2,count,pieces)),
             vmem((width,lines+heads*HD),BF),sem((5,)),sem((max(1,width//min(512,width)),))],
         cost_estimate=pl.CostEstimate(flops=60_000_000_000,bytes_accessed=550_000_000,transcendentals=8_000_000),
         compiler_params=pltpu.CompilerParams(collective_id=cid,has_side_effects=True,vmem_limit_bytes=60*1024*1024),
-    )(cut(grads),cut(two),grad_out,gain,w_out,q,kt,k,v,lse,cosine,sine,segments.reshape(1,length),down,residual,early,mixed,cut(normed),mix)
+    )(cut(grads),cut(two),grad_out,gain,w_out,q,kt,k,v,cosine,sine,down,residual,early,mixed,cut(normed),mix)
 
 
 AXIS="tensor"
@@ -547,28 +569,24 @@
     )(part.reshape(n,rows,D),other.reshape(n,rows,D),tokens,grads,gains,terms)
 
 
-def mlp_kernel(count,pieces,tile,x_hbm,grad_ref,res_ref,early_hbm,wgu_hbm,wd_hbm,
-        part_ref,wide_ref,out_ref,rest_hbm,x_ref,gr,product,gated,lifted,down,ring,tall,sums,total,hs,hr,ss,sr,ws,ts,ls,rs,xs):
-    s=pl.program_id(0)
+def mlp_kernel(count,pieces,tile,grad_ref,res_hbm,x_hbm,early_hbm,wgu_hbm,wd_hbm,
+        out_ref,part_hbm,wide_hbm,rest_hbm,x_ref,gr,product,gated,lifted,down,ring,tall,part_stage,wide_stage,res_ref,sums,total,
+        hs,hr,ss,sr,ws,ts,ls,rs,xs,ps,os):
     length,hidden=product.shape
     width=x_ref.shape[1]
     rows=grad_ref.shape[0]
     half=rows//2
     first,second=hidden//tile,width//tile
     slots=ring.shape[0]
-    at_down=first; at_grad=first+second; at_part=2*first+second; at_weight=2*first+2*second
     begun=early_hbm.shape[1]
     spread=hs.shape[2]
     get=Line(count,spread,rows,held=gr,held_sems=(hs,hr),base=begun,sub=(rows-begun)//spread)
     line=Line(count,pieces,rows,down,sums,(ss,sr),sub=half//pieces)
-    def rest(c): return pltpu.make_async_copy(down.at[c,pl.ds(half,half)],rest_hbm.at[c],rs.at[c])
     def strip(k,size): return pl.ds(pl.multiple_of(jnp.clip(k,0,size-1)*tile,tile),tile)
     def tall_load(k):
         slot=lax.rem(k,slots)
-        @pl.when((k<2*first)&(lax.rem(k,2)==0))
-        def _(): pltpu.make_async_copy(wgu_hbm.at[:,strip(k//2,first)],tall.at[slot],ts.at[slot]).start()
-        @pl.when((k<2*first)&(lax.rem(k,2)==1))
-        def _(): pltpu.make_async_copy(wgu_hbm.at[:,strip(first+k//2,2*first)],tall.at[slot],ts.at[slot]).start()
+        @pl.when(k<2*first)
+        def _(): pltpu.make_async_copy(wgu_hbm.at[:,strip(lax.rem(k,2)*first+k//2,2*first)],tall.at[slot],ts.at[slot]).start()
         @pl.when((k>=2*first)&(k<2*first+second))
         def _(): pltpu.make_async_copy(wd_hbm.at[:,strip(k-2*first,second)],tall.at[slot],ts.at[slot]).start()
     def tall_loaded(k):
@@ -577,61 +595,49 @@
         return slot
     def load(k):
         slot=lax.rem(k,slots)
-        late=strip((k-first)//2,second)
         @pl.when(k<first)
         def _(): pltpu.make_async_copy(wd_hbm.at[strip(k,first),:],ring.at[slot],ws.at[slot]).start()
-        @pl.when((k>=first)&(lax.rem(k-first,2)==0)&(k<first+2*second))
-        def _(): pltpu.make_async_copy(wgu_hbm.at[late,pl.ds(0,hidden)],ring.at[slot],ws.at[slot]).start()
-        @pl.when((k>=first)&(lax.rem(k-first,2)==1)&(k<first+2*second))
-        def _(): pltpu.make_async_copy(wgu_hbm.at[late,pl.ds(hidden,hidden)],ring.at[slot],ws.at[slot]).start()
+        @pl.when((k>=first)&(k<first+2*second))
+        def _():
+            side=pl.ds(pl.multiple_of(lax.rem(k-first,2)*hidden,hidden),hidden)
+            pltpu.make_async_copy(wgu_hbm.at[strip((k-first)//2,second),side],ring.at[slot],ws.at[slot]).start()
     def loaded(k):
         slot=lax.rem(k,slots)
         pltpu.make_async_copy(wd_hbm.at[pl.ds(0,tile),:],ring.at[slot],ws.at[slot]).wait()
         return slot
     def own(): return pltpu.make_async_copy(grad_ref,gr.at[get.here],ls.at[0])
     def early(c): return pltpu.make_async_copy(early_hbm.at[c],gr.at[c,pl.ds(0,begun)],ls.at[1+c])
-    def whole_x(): return pltpu.make_async_copy(x_hbm,x_ref,xs)
-    @pl.when(s==0)
-    def _():
-        whole_x().start()
-        for k in range(slots): tall_load(k)
-        greet(get.here,count)
-        get.gather_step(0,grad_ref)
-        own().start()
-        for c in range(count):
-            @pl.when(c!=get.here)
-            def _(): early(c).start()
-        whole_x().wait()
-    @pl.when(s==at_down-1)
-    def _():
-        for k in range(slots): load(k)
-    hops=get.gather_steps()-1
-    marks=(1,2,3,5,7) if first==4 and second==4 and hops==5 else tuple(min(k+1,at_grad) for k in range(hops))
-    for k,mark in enumerate(marks):
-        @pl.when(s==mark)
-        def _(): get.gather_step(k+1,grad_ref)
-    @pl.when(s==at_grad)
-    def _():
-        own().wait()
-        for c in range(count):
-            @pl.when(c!=get.here)
-            def _(): early(c).wait()
+    def rest(c): return pltpu.make_async_copy(down.at[c,pl.ds(half,half)],rest_hbm.at[c],rs.at[c])
+    whole_x=pltpu.make_async_copy(x_hbm,x_ref,xs)
+    whole_x.start()
+    base=pltpu.make_async_copy(res_hbm.at[pl.ds(0,half)],res_ref,ls.at[1+count])
+    base.start()
+    for k in range(slots): tall_load(jnp.int32(k))
+    greet(get.here,count)
+    get.gather_step(0,grad_ref)
+    own().start()
+    for c in range(count):
+        @pl.when(c!=get.here)
+        def _(): early(c).start()
+    whole_x.wait()
+    hops=get.gather_steps()
+    gather_marks=(1,2,3,5,7) if first==4 and second==4 and hops==6 else tuple(min(k+1,first+second-1) for k in range(hops-1))
+    sum_marks=(0,2,4,5,6,9,12) if first==4 and second==4 and line.far_steps()==7 else tuple(min(k,first+4*second-1) for k in range(line.far_steps()))
+    def gather_at(n):
+        for k,mark in enumerate(gather_marks):
+            @pl.when(n==mark)
+            def _(): get.gather_step(k+1,grad_ref)
     def finish(span,total):
         out_ref[span,:]=(res_ref[span,:]+total[...]).astype(BF)
-    r=s-at_grad
-    t=jnp.int32(-1)
-    marks=(0,2,4,5,6,10,16) if first==4 and second==4 else tuple(range(line.far_steps()))
-    for k,mark in enumerate(marks): t=jnp.where(r==mark,k,t)
-    @pl.when(t>=0)
-    def _(): line.far_step(t,total,finish)
-    @pl.when(r==0)
-    def _():
-        for c in range(count): rest(c).start()
-    @pl.when(s<at_down)
-    def _():
-        one=tall_loaded(2*s)
-        two=tall_loaded(2*s+1)
-        cols=strip(s,first)
+    def sum_at(n):
+        for k,mark in enumerate(sum_marks):
+            @pl.when(n==mark)
+            def _(): line.far_step(jnp.int32(k),total,finish)
+    def forward(n,_):
+        gather_at(n)
+        one=tall_loaded(2*n)
+        two=tall_loaded(2*n+1)
+        cols=strip(n,first)
         for c in range(count):
             span=slice(c*rows,(c+1)*rows)
             gate=jnp.dot(x_ref[span,:],tall[one],preferred_element_type=F32)
@@ -641,88 +647,105 @@
             product[span,cols]=(active*up).astype(BF)
             lifted[span,cols]=active.astype(BF)
             gated[span,cols]=(up*(sigmoid+active*(1.0-sigmoid))).astype(BF)
-        tall_load(2*s+slots)
-        tall_load(2*s+1+slots)
-    @pl.when((s>=at_down)&(s<at_grad))
-    def _():
-        k=2*first+s-at_down
-        slot=tall_loaded(k)
+        tall_load(2*n+slots)
+        tall_load(2*n+1+slots)
+        return 0
+    lax.fori_loop(0,first,forward,0)
+    for k in range(slots): load(jnp.int32(k))
+    def lower(n,_):
+        gather_at(first+n)
+        slot=tall_loaded(2*first+n)
         sums_here=jnp.dot(product[...],tall[slot],preferred_element_type=F32).astype(BF)
-        cols=strip(s-at_down,second)
+        cols=strip(n,second)
         for c in range(count): down[c,:,cols]=sums_here[c*rows:(c+1)*rows]
-        tall_load(k+slots)
-    @pl.when((s>=at_grad)&(s<at_part))
-    def _():
-        k=s-at_grad
-        slot=loaded(k)
-        cols=strip(k,first)
+        tall_load(2*first+n+slots)
+        return 0
+    lax.fori_loop(0,second,lower,0)
+    for c in range(count): rest(c).start()
+    base.wait()
+    own().wait()
+    for c in range(count):
+        @pl.when(c!=get.here)
+        def _(): early(c).wait()
+    def back(n,_):
+        sum_at(n)
+        slot=loaded(n)
+        cols=strip(n,first)
         for c in range(count):
             span=slice(c*rows,(c+1)*rows)
             grads=lax.dot_general(gr[c],ring[slot],(((1,),(1,)),((),())),preferred_element_type=F32)
             gated[span,cols]=(grads*gated[span,cols].astype(F32)).astype(BF)
             lifted[span,cols]=(grads*lifted[span,cols].astype(F32)).astype(BF)
-        load(k+slots)
-    @pl.when((s>=at_part)&(s<at_weight))
-    def _():
-        k=first+2*(s-at_part)
+        load(n+slots)
+        return 0
+    lax.fori_loop(0,first,back,0)
+    def part_copy(n):
+        slot=lax.rem(n,2)
+        return pltpu.make_async_copy(part_stage.at[slot],part_hbm.at[:,strip(n,second)],ps.at[slot])
+    def inner(n,_):
+        sum_at(first+n)
+        k=first+2*n
         one=loaded(k)
         both=lax.dot_general(gated[...],ring[one],(((1,),(1,)),((),())),preferred_element_type=F32)
         load(k+slots)
         two=loaded(k+1)
         both=both+lax.dot_general(lifted[...],ring[two],(((1,),(1,)),((),())),preferred_element_type=F32)
-        part_ref[...]=both.astype(BF)
+        @pl.when(n>=2)
+        def _(): part_copy(n-2).wait()
+        part_stage[lax.rem(n,2)]=both.astype(BF)
+        part_copy(n).start()
         load(k+1+slots)
-    last=s-at_weight
-    cols=strip(last//6,second)
-    kind=lax.rem(last,6)
+        return 0
+    lax.fori_loop(0,second,inner,0)
+    def wide_copy(n):
+        slot=lax.rem(n,2)
+        side=pl.ds(pl.multiple_of(lax.rem(n,3)*hidden,hidden),hidden)
+        return pltpu.make_async_copy(wide_stage.at[slot],wide_hbm.at[strip(n//3,second),side],os.at[slot])
     cut=hidden//2
-    def weight(left,right):
-        wide_ref[...]=lax.dot_general(left,right,(((0,),(0,)),((),())),preferred_element_type=F32).astype(BF)
-    for side in (0,1):
-        these=slice(side*cut,(side+1)*cut)
-        @pl.when((last>=0)&(kind==side))
-        def _(): weight(x_ref[:,cols],gated[:,these])
-        @pl.when((last>=0)&(kind==2+side))
-        def _(): weight(x_ref[:,cols],lifted[:,these])
-        @pl.when((last>=0)&(kind==4+side))
-        def _(): weight(gr[:,:,cols].reshape(length,tile),product[:,these])
-    @pl.when(s==at_weight+6*second-1)
-    def _():
-        get.end_pieces()
-        line.end_sums()
-        for c in range(count): rest(c).wait()
+    def weights(m,_):
+        cols=strip(m,second)
+        for kind in range(3):
+            n=3*m+kind
+            sum_at(first+second+n)
+            @pl.when(n>=2)
+            def _(): wide_copy(n-2).wait()
+            left=gr[:,:,cols].reshape(length,tile) if kind==2 else x_ref[:,cols]
+            right=(gated,lifted,product)[kind]
+            for side in (0,1):
+                these=slice(side*cut,(side+1)*cut)
+                wide_stage[lax.rem(n,2),:,these]=lax.dot_general(left,right[:,these],(((0,),(0,)),((),())),preferred_element_type=F32).astype(BF)
+            wide_copy(n).start()
+        return 0
+    lax.fori_loop(0,second,weights,0)
+    get.end_pieces()
+    line.end_sums()
+    for c in range(count): rest(c).wait()
+    for n in range(max(0,second-2),second): part_copy(jnp.int32(n)).wait()
+    for n in range(3*second-2,3*second): wide_copy(jnp.int32(n)).wait()
 
 def mlp(x,grad_out,residual,early,w_both,w_down,cid,spread,pieces,count):
     length,width=x.shape
     hidden=w_down.shape[0]
     rows=length//count
     tile=min(512,hidden,width)
-    first,second=hidden//tile,width//tile
-    steps=2*first+8*second
-    assert first!=4 or second!=4 or (count-1)*pieces+1==7
-    assert first+7*second>=(count-1)*pieces+1
-    whole=lambda shape: pl.BlockSpec(shape,lambda s: (0,)*len(shape),pipeline_mode=pl.Buffered(1))
+    vm=pl.BlockSpec(memory_space=pltpu.VMEM)
     hbm=pl.BlockSpec(memory_space=pl.ANY)
     sds=jax.ShapeDtypeStruct
     sem=pltpu.SemaphoreType.DMA
-    at_part=2*first+second
-    def wide_map(s):
-        k=jnp.maximum(s-at_part-second,0)
-        return (k//6,k%6)
     vmem=pltpu.VMEM
+    half=rows//2
     return pl.pallas_call(functools.partial(mlp_kernel,count,pieces,tile),
-        grid=(steps,),
-        out_shape=(sds((length,width),BF),sds((width,3*hidden),BF),sds((rows//2,width),BF),sds((count,rows//2,width),BF)),
-        in_specs=[hbm,whole((rows,width)),pl.BlockSpec((rows//2,width),lambda s: (0,0),pipeline_mode=pl.Buffered(1)),hbm,hbm,hbm],
-        out_specs=(pl.BlockSpec((length,tile),lambda s: (0,jnp.clip(s-at_part,0,second-1))),
-            pl.BlockSpec((tile,hidden//2),wide_map),whole((rows//2,width)),hbm),
+        out_shape=(sds((half,width),BF),sds((length,width),BF),sds((width,3*hidden),BF),sds((count,half,width),BF)),
+        in_specs=[vm,hbm,hbm,hbm,hbm,hbm],
+        out_specs=(vm,hbm,hbm,hbm),
         scratch_shapes=[vmem((length,width),BF),vmem((count,rows,width),BF),vmem((length,hidden),BF),vmem((length,hidden),BF),vmem((length,hidden),BF),
-            vmem((count,rows,width),BF),vmem((4,tile,width),BF),vmem((4,width,tile),BF),vmem((count+1,rows//2,width),BF),vmem((rows//2//pieces,width),F32),
-            sem((2,count,spread)),sem((2,count,spread)),sem((2,count,pieces)),sem((2,count,pieces)),sem((4,)),sem((4,)),sem((count+1,)),sem((count,)),sem],
+            vmem((count,rows,width),BF),vmem((4,tile,width),BF),vmem((4,width,tile),BF),vmem((2,length,tile),BF),vmem((2,tile,hidden),BF),vmem((half,width),F32),
+            vmem((count+1,half,width),BF),vmem((half//pieces,width),F32),
+            sem((2,count,spread)),sem((2,count,spread)),sem((2,count,pieces)),sem((2,count,pieces)),sem((4,)),sem((4,)),sem((count+2,)),sem((count,)),sem,
+            sem((2,)),sem((2,))],
         cost_estimate=pl.CostEstimate(flops=78_000_000_000,bytes_accessed=380_000_000,transcendentals=0),
-        compiler_params=pltpu.CompilerParams(collective_id=cid,has_side_effects=True,vmem_limit_bytes=60*1024*1024,
-            dimension_semantics=("arbitrary",)),
-    )(x,grad_out,residual,early,w_both,w_down)
+        compiler_params=pltpu.CompilerParams(collective_id=cid,has_side_effects=True,vmem_limit_bytes=60*1024*1024),
+    )(grad_out,residual,x,early,w_both,w_down)
 
 
 def frequencies(head_size):
@@ -935,14 +958,14 @@
     normed_one, gains, both, cosine, sine = norm_and_gather(tokens, own_gains, w_gate, w_up, angles, 1, 4, count, plane)
     full_both = lax.all_gather(both, DP, axis=0, tiled=True)
 
-    mixed, lse, q, kt, k, v, residual, early, normed_two = attend(
+    mixed, q, kt, k, v, residual, early, normed_two = attend(
         mix, normed_one, cosine, sine, segments, full_out, grad_out, tokens, gains, heads, groups, 6, rows * 5 // 8, 5, 16, count
     )
     normed_two = normed_two.reshape(count * rows, width)
-    part, grad_wide, block_early, down = mlp(normed_two, grad_out, residual, early, full_both, full_down, 5, 3, 2, count)
+    block_early, part, grad_wide, down = mlp(normed_two, grad_out, residual, early, full_both, full_down, 5, 3, 2, count)
     grad_wide = lax.psum_scatter(grad_wide, DP, scatter_dimension=0, tiled=True)
     grad_residual, terms_two, part, grad_mix, block_out = attend_back(
-        part, normed_two, grad_out, gains, full_out, q, kt, k, v, lse, cosine, sine, segments, down, residual, block_early,
+        part, normed_two, grad_out, gains, full_out, q, kt, k, v, cosine, sine, down, residual, block_early,
         mixed, normed_one, mix, heads, groups, 7, 2, 16, count,
     )
     grad_mix = lax.psum_scatter(grad_mix, DP, scatter_dimension=0, tiled=True)

time: 605 us -> 590 us (0.975)
  Pallas kernels: 575 us -> 559 us
    pallas_call x1, Pallas kernels: 108 us -> 98.5 us  [mlp(): pl.pallas_call(functools.partial(mlp_kernel, count, pieces, tile), out_sh...]
    pallas_call x1, Pallas kernels: 159 us -> 152 us  [attend_back(): pl.pallas_call(functools.partial(attend_back_kernel, heads, groups, block...]
  transfers between devices with their start and end apart: 6 -> 6, of which waited for: 0 -> 0; matrix products, arithmetic and copies ran while one was open for 1% -> 1% of each run, Pallas kernels for 78% -> 79%
where the time goes in v1:
time: 590 us; the launch traced here: 581 us
  Pallas kernels  559 us (95%)
  between operations  14.7 us (2%)
    pallas_call x1, Pallas kernels, attend_back(): pl.pallas_call(functools.partial(attend_back_kernel, heads, groups, block...  152 us
    pallas_call x1, Pallas kernels, attend(): pl.pallas_call(functools.partial(attend_kernel, heads, groups, block, cou...  148 us
    pallas_call x1, Pallas kernels, mlp(): pl.pallas_call(functools.partial(mlp_kernel, count, pieces, tile), out_sh...  98.5 us
    pallas_call x1, Pallas kernels, norm_and_gather(): pl.pallas_call(functools.partial(norm_kernel, count, plane, pieces), out_...  77.6 us
    pallas_call x1, Pallas kernels, last_sums(): pl.pallas_call(functools.partial(last_kernel, n, plane, pieces), out_shap...  73.8 us
  transfers between devices with their start and end apart: 6, of which 0 were waited for; matrix products, arithmetic and copies ran while one was open for 1% of the time, Pallas kernels for 79%

profile of v1, /device:TPU:0, one launch (start us, length us, event | category | flops | bytes accessed | tf_op | source)
XLA Modules:
  0.0 580.9 jit_solution(3286988297176894055)
XLA Ops:
  7.2 0.0 all-gather.7.cloned.1.call-start
  7.2 0.7 all-gather.7.cloned.1.call-update
  7.9 0.0 all-gather.5.cloned.1.call-start
  8.0 1.8 pad_maximum_fusion
  9.8 0.0 all-gather.5.cloned.1.call-update
  9.8 0.0 all-gather.11.cloned.1.call-start
  9.8 0.7 all-gather.11.cloned.1.call-update
  10.5 0.0 all-gather.9.cloned.1.call-start
  10.6 0.7 stack.9
  11.2 0.7 stack.10
  11.9 0.7 convert_element_type.4
  12.6 0.6 fusion.3.gains_ref
  13.2 0.7 broadcast_multiply_fusion.angles_ref
  13.9 77.6 %shard_map.212 = (bf16[4,256,2048]{2,1,0:T(8,128)(2,1)}, f32[8,2048]{1,0:T(8,128)}, bf16[256,4096]{1,0:T(8,128)(2,1)}, f32[32,1024]{1,0:T(8,128)}, f32[32,1024]{1,0:T(8,128)}) custom-call(bf16[256,2048]{1,0:T(8,128)(2,1)} %tokens_hbm.3, f32[8,256]{1,0:T(8,128)} %fusion.3.gains_ref, bf16[256,2048]{1,0:T(8,128)(2,1)} %gate_hbm.1, bf16[256,2048]{1,0:T(8,128)(2,1)} %up_hbm.1, ...), custom_call_target="tpu_custom_call" | custom-call | bytes 270000000 | tf_op jit(solution)/shard_map/pallas_call | solution.py:827
  91.6 0.0 all-gather.9.cloned.1.call-update
  91.6 0.0 reduce-scatter.3.cloned.1.call-start
  91.6 0.0 all-gather.7.cloned.1.call-done.wo_hbm
  91.7 0.0 all-gather.5.cloned.1.call-done.mix_hbm
  91.7 148.0 %shard_map.213 = (bf16[512,1024]{1,0:T(8,128)(2,1)}, bf16[8,80,1024]{2,1,0:T(8,128)(2,1)}, bf16[128,1024]{1,0:T(8,128)(2,1)}, bf16[2,1024,80]{2,1,0:T(8,128)(2,1...) custom-call(bf16[2048,768]{1,0:T(8,128)(2,1)} %all-gather.5.cloned.1, ...), custom_call_target="tpu_custom_call" | custom-call | flops 30000001024 | bytes 500000000 | tf_op jit(solution)/shard_map/pallas_call | solution.py:152
  239.7 0.0 all-gather.11.cloned.1.call-done.wd_hbm
  239.8 0.0 all-gather.9.cloned.1.call-done.wgu_hbm
  239.8 98.5 %shard_map.214 = (bf16[128,2048]{1,0:T(8,128)(2,1)}, bf16[1024,2048]{1,0:T(8,128)(2,1)}, bf16[2048,6144]{1,0:T(8,128)(2,1)}, bf16[4,128,2048]{2,1,0:T(8,128)(2,1)}) custom-call(bf16[256,2048]{1,0:T(8,128)(2,1)} %go_ref.1, f32[256,2048]{1,0:T(8,128)} %get-tuple-element.51.res_hbm.res_ref, bf16[1024,2048]{1,0:T(8,128)(2,1)} %bitcast.10, ...), custom_call_target="tpu_custom_call" | custom-call | flops 77999996928 | bytes 380000000 | tf_op jit(solution)/shard_map/pallas_call | solution.py:737
  338.3 0.0 reduce-scatter.3.cloned.1.call-update
  338.3 0.0 reduce-scatter.5.cloned.1.call-start
  338.4 152.3 %shard_map.215 = (f32[256,2048]{1,0:T(8,128)}, f32[8,2048]{1,0:T(8,128)}, bf16[4,256,2048]{2,1,0:T(8,128)(2,1)}, bf16[2048,1280]{1,0:T(8,128)(2,1)}, bf16[256,2048]{1,0:T(8,128)(2,1)}) custom-call(bf16[4,256,2048]{2,1,0:T(8,128)(2,1)} %bitcast.11, bf16[4,256,2048]{2,1,0:T(8,128)(2,1)} %get-tuple-element.52.two_hbm, bf16[256,2048]{1,0:T(8,128)(2,1)} %go_ref.1, ...), custom_call_target="tpu_custom_call" | custom-call | flops 60000002048 | bytes 550000000 | tf_op jit(solution)/shard_map/pallas_call | solution.py:315
  490.7 0.0 reduce-scatter.5.cloned.1.call-update
  490.7 73.8 %shard_map.216 = (f32[256,2048]{1,0:T(8,128)}, f32[16,256]{1,0:T(8,128)}) custom-call(bf16[4,256,2048]{2,1,0:T(8,128)(2,1)} %get-tuple-element.64.part_hbm, bf16[4,256,2048]{2,1,0:T(8,128)(2,1)} %get-tuple-element.47.normed_hbm.other_hbm, bf16[256,2048]{1,0:T(8,128)(2,1)} %tokens_hbm.3, f32[256,2048]{1,0:T(8,128)} %get-tuple-element.65.grads_hbm, ...), custom_call_target="tpu_custom_call" | custom-call | bytes 270000000 | tf_op jit(solution)/shard_map/pallas_call | solution.py:562
  564.5 0.0 reduce-scatter.3.cloned.1.call-done.gate_in.up_in.down_in
  564.6 6.8 %shard_map.217 = (f32[256,2048]{1,0:T(8,128)}, f32[256,2048]{1,0:T(8,128)}, f32[2048,256]{1,0:T(8,128)}, f32[256,2048]{1,0:T(8,128)}, bf16[256,2048]{1,0:T(8,128)(2,1)}, /*index=5*/f32[2,256]{1,0:T(2,128)}) custom-call(bf16[256,6144]{1,0:T(8,128)(2,1)} %reduce-scatter.3.cloned.1.call-done.gate_in.up_in.down_in, ...), custom_call_target="tpu_custom_call" | custom-call | tf_op jit(solution)/shard_map/pallas_call | solution.py:874
  571.4 0.0 reduce-scatter.5.cloned.1.call-done.mix_ref
  571.4 2.2 shard_map.218
  (1 shorter events, 0.0 us)
Async XLA Ops:
  7.2 84.5 %all-gather.7.cloned.1.call-start = ((), (), s32[]{:S(2)}) async-start(), calls=%async_computation.3 | async-start | bytes 2359296 | tf_op jit(solution)/shard_map/all_gather | solution.py:953
  7.9 83.8 %all-gather.5.cloned.1.call-start = ((), (), s32[]{:S(2)}) async-start(), calls=%async_computation.2 | async-start | bytes 3538944 | tf_op jit(solution)/shard_map/all_gather | solution.py:952
  9.8 230.0 %all-gather.11.cloned.1.call-start = ((), (), s32[]{:S(2)}) async-start(), calls=%async_computation.5 | async-start | bytes 9437184 | tf_op jit(solution)/shard_map/all_gather | solution.py:954
  10.5 229.2 %all-gather.9.cloned.1.call-start = ((), (), s32[]{:S(2)}) async-start(), calls=%async_computation.4 | async-start | bytes 18874368 | tf_op jit(solution)/shard_map/all_gather | solution.py:959
  91.6 473.0 %reduce-scatter.3.cloned.1.call-start = ((), (), s32[]{:S(2)}) async-start(), calls=%async_computation.6 | async-start | bytes 28311552 | tf_op jit(solution)/shard_map/reduce_scatter | solution.py:966
  338.3 233.1 %reduce-scatter.5.cloned.1.call-start = ((), (), s32[]{:S(2)}) async-start(), calls=%async_computation.7 | async-start | bytes 5898240 | tf_op jit(solution)/shard_map/reduce_scatter | solution.py:971
Sparse Core Ops, SparseCore 0:
  9.9 30.8 all-gather.6
  43.3 32.3 all-gather.4
  77.5 56.0 all-gather.10
  135.3 89.8 all-gather.8
  338.5 163.9 reduce-scatter.2
  505.7 56.9 reduce-scatter.4

commit v2 on v1

--- a/solution.py
+++ b/solution.py
@@ -64,7 +64,6 @@
         if done+1<steps:
             done+=1
             line.gather_step(done,grad_ref)
-    tick()
     cosine, sine = cos_ref[...], sin_ref[...]
     segs=segr_ref[...]
     apart=[jnp.where(segs==s,MASKED,0.0).astype(F32) for s in range(3)]
@@ -89,7 +88,7 @@
     tri_ref[...]=triangle(block)
     for start in range(0,length,block):
         cols=slice(start,start+block)
-        if start in (block,3*block): tick()
+        if start in (0,2*block): tick()
         def head(h,_):
             g=h//per
             rows=pl.ds(pl.multiple_of(h*HD,HD),HD)
@@ -621,12 +620,13 @@
         def _(): early(c).start()
     whole_x.wait()
     hops=get.gather_steps()
-    gather_marks=(1,2,3,5,7) if first==4 and second==4 and hops==6 else tuple(min(k+1,first+second-1) for k in range(hops-1))
-    sum_marks=(0,2,4,5,6,9,12) if first==4 and second==4 and line.far_steps()==7 else tuple(min(k,first+4*second-1) for k in range(line.far_steps()))
-    def gather_at(n):
+    gather_marks=(1.5,2.75,4,6,8) if first==4 and second==4 and hops==6 else tuple(min(k+1,first+second) for k in range(hops-1))
+    sum_marks=(0,3,5,6,7,9,12) if first==4 and second==4 and line.far_steps()==7 else tuple(min(k,first+4*second-1) for k in range(line.far_steps()))
+    def gather_at(n,after=0.0):
         for k,mark in enumerate(gather_marks):
-            @pl.when(n==mark)
-            def _(): get.gather_step(k+1,grad_ref)
+            if mark%1==after:
+                @pl.when(n==int(mark))
+                def _(): get.gather_step(k+1,grad_ref)
     def finish(span,total):
         out_ref[span,:]=(res_ref[span,:]+total[...]).astype(BF)
     def sum_at(n):
@@ -639,6 +639,7 @@
         two=tall_loaded(2*n+1)
         cols=strip(n,first)
         for c in range(count):
+            if c: gather_at(n,c/count)
             span=slice(c*rows,(c+1)*rows)
             gate=jnp.dot(x_ref[span,:],tall[one],preferred_element_type=F32)
             up=jnp.dot(x_ref[span,:],tall[two],preferred_element_type=F32)
@@ -662,6 +663,7 @@
         return 0
     lax.fori_loop(0,second,lower,0)
     for c in range(count): rest(c).start()
+    gather_at(jnp.int32(first+second))
     base.wait()
     own().wait()
     for c in range(count):
@@ -795,7 +797,15 @@
         give(c, u).start()
 
     def step(t, _):
-        line.pass_pieces(t, lambda c, u: norm(held[c, line.span(u)], c, u))
+        line.pass_pieces(t)
+        for k in range(1, count):
+            u = t - k
+            for c in (line.here - k, line.here + k):
+
+                @pl.when(line.fits(u) & (c >= 0) & (c < count))
+                def _():
+                    place, piece = jnp.clip(c, 0, count - 1), jnp.clip(u, 0, pieces - 1)
+                    norm(held[place, line.span(piece)], place, piece)
 
         @pl.when(t == 1)
         def _():

time: 590 us -> 583 us (0.988)
  Pallas kernels: 559 us -> 553 us
where the time goes in v2:
time: 583 us; the launch traced here: 575 us
  Pallas kernels  553 us (95%)
  between operations  14.7 us (3%)
    pallas_call x1, Pallas kernels, attend_back(): pl.pallas_call(functools.partial(attend_back_kernel, heads, groups, block...  149 us
    pallas_call x1, Pallas kernels, attend(): pl.pallas_call(functools.partial(attend_kernel, heads, groups, block, cou...  146 us
    pallas_call x1, Pallas kernels, mlp(): pl.pallas_call(functools.partial(mlp_kernel, count, pieces, tile), out_sh...  98.3 us
    pallas_call x1, Pallas kernels, norm_and_gather(): pl.pallas_call(functools.partial(norm_kernel, count, plane, pieces), out_...  77.6 us
    pallas_call x1, Pallas kernels, last_sums(): pl.pallas_call(functools.partial(last_kernel, n, plane, pieces), out_shap...  72.4 us
  transfers between devices with their start and end apart: 6, of which 0 were waited for; matrix products, arithmetic and copies ran while one was open for 1% of the time, Pallas kernels for 79%

profile of v2, /device:TPU:0, one launch (start us, length us, event | category | flops | bytes accessed | tf_op | source)
XLA Modules:
  0.0 574.6 jit_solution(13571882497385177270)
XLA Ops:
  7.2 0.0 all-gather.7.cloned.1.call-start
  7.2 0.7 all-gather.7.cloned.1.call-update
  7.9 0.0 all-gather.5.cloned.1.call-start
  8.0 1.8 pad_maximum_fusion
  9.8 0.0 all-gather.5.cloned.1.call-update
  9.8 0.0 all-gather.11.cloned.1.call-start
  9.8 0.7 all-gather.11.cloned.1.call-update
  10.5 0.0 all-gather.9.cloned.1.call-start
  10.6 0.7 stack.9
  11.2 0.7 stack.10
  11.9 0.7 convert_element_type.4
  12.6 0.6 fusion.3.gains_ref
  13.2 0.7 broadcast_multiply_fusion.angles_ref
  13.9 77.6 %shard_map.212 = (bf16[4,256,2048]{2,1,0:T(8,128)(2,1)}, f32[8,2048]{1,0:T(8,128)}, bf16[256,4096]{1,0:T(8,128)(2,1)}, f32[32,1024]{1,0:T(8,128)}, f32[32,1024]{1,0:T(8,128)}) custom-call(bf16[256,2048]{1,0:T(8,128)(2,1)} %tokens_hbm.3, f32[8,256]{1,0:T(8,128)} %fusion.3.gains_ref, bf16[256,2048]{1,0:T(8,128)(2,1)} %gate_hbm.1, bf16[256,2048]{1,0:T(8,128)(2,1)} %up_hbm.1, ...), custom_call_target="tpu_custom_call" | custom-call | bytes 270000000 | tf_op jit(solution)/shard_map/pallas_call | solution.py:837
  91.6 0.0 all-gather.9.cloned.1.call-update
  91.6 0.0 reduce-scatter.3.cloned.1.call-start
  91.6 0.0 all-gather.7.cloned.1.call-done.wo_hbm
  91.7 0.0 all-gather.5.cloned.1.call-done.mix_hbm
  91.7 146.1 %shard_map.213 = (bf16[512,1024]{1,0:T(8,128)(2,1)}, bf16[8,80,1024]{2,1,0:T(8,128)(2,1)}, bf16[128,1024]{1,0:T(8,128)(2,1)}, bf16[2,1024,80]{2,1,0:T(8,128)(2,1...) custom-call(bf16[2048,768]{1,0:T(8,128)(2,1)} %all-gather.5.cloned.1, ...), custom_call_target="tpu_custom_call" | custom-call | flops 30000001024 | bytes 500000000 | tf_op jit(solution)/shard_map/pallas_call | solution.py:151
  237.8 0.0 all-gather.11.cloned.1.call-done.wd_hbm
  237.8 0.0 all-gather.9.cloned.1.call-done.wgu_hbm
  237.9 98.3 %shard_map.214 = (bf16[128,2048]{1,0:T(8,128)(2,1)}, bf16[1024,2048]{1,0:T(8,128)(2,1)}, bf16[2048,6144]{1,0:T(8,128)(2,1)}, bf16[4,128,2048]{2,1,0:T(8,128)(2,1)}) custom-call(bf16[256,2048]{1,0:T(8,128)(2,1)} %go_ref.1, f32[256,2048]{1,0:T(8,128)} %get-tuple-element.51.res_hbm.res_ref, bf16[1024,2048]{1,0:T(8,128)(2,1)} %bitcast.10, ...), custom_call_target="tpu_custom_call" | custom-call | flops 77999996928 | bytes 380000000 | tf_op jit(solution)/shard_map/pallas_call | solution.py:739
  336.2 0.0 reduce-scatter.3.cloned.1.call-update
  336.2 0.0 reduce-scatter.5.cloned.1.call-start
  336.3 149.4 %shard_map.215 = (f32[256,2048]{1,0:T(8,128)}, f32[8,2048]{1,0:T(8,128)}, bf16[4,256,2048]{2,1,0:T(8,128)(2,1)}, bf16[2048,1280]{1,0:T(8,128)(2,1)}, bf16[256,2048]{1,0:T(8,128)(2,1)}) custom-call(bf16[4,256,2048]{2,1,0:T(8,128)(2,1)} %bitcast.11, bf16[4,256,2048]{2,1,0:T(8,128)(2,1)} %get-tuple-element.52.two_hbm, bf16[256,2048]{1,0:T(8,128)(2,1)} %go_ref.1, ...), custom_call_target="tpu_custom_call" | custom-call | flops 60000002048 | bytes 550000000 | tf_op jit(solution)/shard_map/pallas_call | solution.py:314
  485.7 0.0 reduce-scatter.5.cloned.1.call-update
  485.7 72.4 %shard_map.216 = (f32[256,2048]{1,0:T(8,128)}, f32[16,256]{1,0:T(8,128)}) custom-call(bf16[4,256,2048]{2,1,0:T(8,128)(2,1)} %get-tuple-element.64.part_hbm, bf16[4,256,2048]{2,1,0:T(8,128)(2,1)} %get-tuple-element.47.normed_hbm.other_hbm, bf16[256,2048]{1,0:T(8,128)(2,1)} %tokens_hbm.3, f32[256,2048]{1,0:T(8,128)} %get-tuple-element.65.grads_hbm, ...), custom_call_target="tpu_custom_call" | custom-call | bytes 270000000 | tf_op jit(solution)/shard_map/pallas_call | solution.py:561
  558.1 0.0 reduce-scatter.3.cloned.1.call-done.gate_in.up_in.down_in
  558.2 6.8 %shard_map.217 = (f32[256,2048]{1,0:T(8,128)}, f32[256,2048]{1,0:T(8,128)}, f32[2048,256]{1,0:T(8,128)}, f32[256,2048]{1,0:T(8,128)}, bf16[256,2048]{1,0:T(8,128)(2,1)}, /*index=5*/f32[2,256]{1,0:T(2,128)}) custom-call(bf16[256,6144]{1,0:T(8,128)(2,1)} %reduce-scatter.3.cloned.1.call-done.gate_in.up_in.down_in, ...), custom_call_target="tpu_custom_call" | custom-call | tf_op jit(solution)/shard_map/pallas_call | solution.py:884
  565.0 0.0 reduce-scatter.5.cloned.1.call-done.mix_ref
  565.0 2.2 shard_map.218
  (1 shorter events, 0.0 us)
Async XLA Ops:
  7.2 84.5 %all-gather.7.cloned.1.call-start = ((), (), s32[]{:S(2)}) async-start(), calls=%async_computation.3 | async-start | bytes 2359296 | tf_op jit(solution)/shard_map/all_gather | solution.py:963
  7.9 83.8 %all-gather.5.cloned.1.call-start = ((), (), s32[]{:S(2)}) async-start(), calls=%async_computation.2 | async-start | bytes 3538944 | tf_op jit(solution)/shard_map/all_gather | solution.py:962
  9.8 228.0 %all-gather.11.cloned.1.call-start = ((), (), s32[]{:S(2)}) async-start(), calls=%async_computation.5 | async-start | bytes 9437184 | tf_op jit(solution)/shard_map/all_gather | solution.py:964
  10.5 227.3 %all-gather.9.cloned.1.call-start = ((), (), s32[]{:S(2)}) async-start(), calls=%async_computation.4 | async-start | bytes 18874368 | tf_op jit(solution)/shard_map/all_gather | solution.py:969
  91.6 466.6 %reduce-scatter.3.cloned.1.call-start = ((), (), s32[]{:S(2)}) async-start(), calls=%async_computation.6 | async-start | bytes 28311552 | tf_op jit(solution)/shard_map/reduce_scatter | solution.py:976
  336.2 228.8 %reduce-scatter.5.cloned.1.call-start = ((), (), s32[]{:S(2)}) async-start(), calls=%async_computation.7 | async-start | bytes 5898240 | tf_op jit(solution)/shard_map/reduce_scatter | solution.py:981
Sparse Core Ops, SparseCore 0:
  9.9 30.8 all-gather.6
  43.3 32.3 all-gather.4
  77.5 56.0 all-gather.10
  135.3 89.9 all-gather.8
  336.3 157.3 reduce-scatter.2
  496.9 56.9 reduce-scatter.4

commit v3 on v2

--- a/solution.py
+++ b/solution.py
@@ -620,7 +620,7 @@
         def _(): early(c).start()
     whole_x.wait()
     hops=get.gather_steps()
-    gather_marks=(1.5,2.75,4,6,8) if first==4 and second==4 and hops==6 else tuple(min(k+1,first+second) for k in range(hops-1))
+    gather_marks=(1.5,2.75,4.0,6.0,7.0,8.0) if first==4 and second==4 and hops==7 else tuple(min(k+1,first+second) for k in range(hops-1))
     sum_marks=(0,3,5,6,7,9,12) if first==4 and second==4 and line.far_steps()==7 else tuple(min(k,first+4*second-1) for k in range(line.far_steps()))
     def gather_at(n,after=0.0):
         for k,mark in enumerate(gather_marks):
@@ -969,10 +969,10 @@
     full_both = lax.all_gather(both, DP, axis=0, tiled=True)
 
     mixed, q, kt, k, v, residual, early, normed_two = attend(
-        mix, normed_one, cosine, sine, segments, full_out, grad_out, tokens, gains, heads, groups, 6, rows * 5 // 8, 5, 16, count
+        mix, normed_one, cosine, sine, segments, full_out, grad_out, tokens, gains, heads, groups, 6, rows // 2, 4, 16, count
     )
     normed_two = normed_two.reshape(count * rows, width)
-    block_early, part, grad_wide, down = mlp(normed_two, grad_out, residual, early, full_both, full_down, 5, 3, 2, count)
+    block_early, part, grad_wide, down = mlp(normed_two, grad_out, residual, early, full_both, full_down, 5, 4, 2, count)
     grad_wide = lax.psum_scatter(grad_wide, DP, scatter_dimension=0, tiled=True)
     grad_residual, terms_two, part, grad_mix, block_out = attend_back(
         part, normed_two, grad_out, gains, full_out, q, kt, k, v, cosine, sine, down, residual, block_early,

time: 583 us -> 583 us (level)
    pallas_call x1, Pallas kernels: 146 us -> 140 us  [attend(): pl.pallas_call(functools.partial(attend_kernel, heads, groups, block, cou...]
  transfers between devices with their start and end apart: 6 -> 6, of which waited for: 0 -> 0; matrix products, arithmetic and copies ran while one was open for 1% -> 1% of each run, Pallas kernels for 79% -> 78%
where the time goes in v3:
time: 583 us; the launch traced here: 574 us
  Pallas kernels  555 us (95%)
  between operations  14.7 us (3%)
    pallas_call x1, Pallas kernels, attend_back(): pl.pallas_call(functools.partial(attend_back_kernel, heads, groups, block...  151 us
    pallas_call x1, Pallas kernels, attend(): pl.pallas_call(functools.partial(attend_kernel, heads, groups, block, cou...  140 us
    pallas_call x1, Pallas kernels, mlp(): pl.pallas_call(functools.partial(mlp_kernel, count, pieces, tile), out_sh...  104 us
    pallas_call x1, Pallas kernels, norm_and_gather(): pl.pallas_call(functools.partial(norm_kernel, count, plane, pieces), out_...  77.6 us
    pallas_call x1, Pallas kernels, last_sums(): pl.pallas_call(functools.partial(last_kernel, n, plane, pieces), out_shap...  73.1 us
  transfers between devices with their start and end apart: 6, of which 0 were waited for; matrix products, arithmetic and copies ran while one was open for 1% of the time, Pallas kernels for 78%

profile of v3, /device:TPU:0, one launch (start us, length us, event | category | flops | bytes accessed | tf_op | source)
XLA Modules:
  0.0 574.3 jit_solution(14994348010207294917)
XLA Ops:
  7.2 0.0 copy-start.1
  7.2 0.0 copy-start.2
  7.2 0.0 copy-start
  7.2 0.0 all-gather.7.cloned.1.call-start
  7.3 0.7 all-gather.7.cloned.1.call-update
  7.9 0.0 all-gather.5.cloned.1.call-start
  8.0 1.8 pad_maximum_fusion
  9.8 0.0 all-gather.5.cloned.1.call-update
  9.8 0.0 all-gather.11.cloned.1.call-start
  9.9 0.7 all-gather.11.cloned.1.call-update
  10.6 0.0 all-gather.9.cloned.1.call-start
  10.6 0.0 copy-done.1
  10.6 0.0 copy-done.2
  10.7 0.0 copy-done
  10.7 0.6 fusion.3.gains_ref
  11.3 0.7 broadcast_multiply_fusion.angles_ref
  12.0 77.6 %shard_map.212 = (bf16[4,256,2048]{2,1,0:T(8,128)(2,1)}, f32[8,2048]{1,0:T(8,128)}, bf16[256,4096]{1,0:T(8,128)(2,1)}, f32[32,1024]{1,0:T(8,128)}, f32[32,1024]{1,0:T(8,128)}) custom-call(bf16[256,2048]{1,0:T(8,128)(2,1)} %tokens_hbm.3, f32[8,256]{1,0:T(8,128)} %fusion.3.gains_ref, bf16[256,2048]{1,0:T(8,128)(2,1)} %gate_hbm.1, bf16[256,2048]{1,0:T(8,128)(2,1)} %up_hbm.1, ...), custom_call_target="tpu_custom_call" | custom-call | bytes 270000000 | tf_op jit(solution)/shard_map/pallas_call | solution.py:837
  89.6 0.0 all-gather.9.cloned.1.call-update
  89.7 0.0 reduce-scatter.3.cloned.1.call-start
  89.7 0.0 all-gather.7.cloned.1.call-done.wo_hbm
  89.7 0.0 all-gather.5.cloned.1.call-done.mix_hbm
  89.8 140.0 %shard_map.213 = (bf16[512,1024]{1,0:T(8,128)(2,1)}, bf16[8,80,1024]{2,1,0:T(8,128)(2,1)}, bf16[128,1024]{1,0:T(8,128)(2,1)}, bf16[2,1024,80]{2,1,0:T(8,128)(2,1...) custom-call(bf16[2048,768]{1,0:T(8,128)(2,1)} %all-gather.5.cloned.1, ...), custom_call_target="tpu_custom_call" | custom-call | flops 30000001024 | bytes 500000000 | tf_op jit(solution)/shard_map/pallas_call | solution.py:151
  229.8 0.0 all-gather.11.cloned.1.call-done.wd_hbm
  229.8 0.0 all-gather.9.cloned.1.call-done.wgu_hbm
  229.9 104.1 %shard_map.214 = (bf16[128,2048]{1,0:T(8,128)(2,1)}, bf16[1024,2048]{1,0:T(8,128)(2,1)}, bf16[2048,6144]{1,0:T(8,128)(2,1)}, bf16[4,128,2048]{2,1,0:T(8,128)(2,1)}) custom-call(bf16[256,2048]{1,0:T(8,128)(2,1)} %go_ref.1, f32[256,2048]{1,0:T(8,128)} %get-tuple-element.51.res_hbm.res_ref, bf16[1024,2048]{1,0:T(8,128)(2,1)} %bitcast.10, ...), custom_call_target="tpu_custom_call" | custom-call | flops 77999996928 | bytes 380000000 | tf_op jit(solution)/shard_map/pallas_call | solution.py:739
  334.0 0.0 reduce-scatter.3.cloned.1.call-update
  334.0 0.0 reduce-scatter.5.cloned.1.call-start
  334.1 150.6 %shard_map.215 = (f32[256,2048]{1,0:T(8,128)}, f32[8,2048]{1,0:T(8,128)}, bf16[4,256,2048]{2,1,0:T(8,128)(2,1)}, bf16[2048,1280]{1,0:T(8,128)(2,1)}, bf16[256,2048]{1,0:T(8,128)(2,1)}) custom-call(bf16[4,256,2048]{2,1,0:T(8,128)(2,1)} %bitcast.11, bf16[4,256,2048]{2,1,0:T(8,128)(2,1)} %get-tuple-element.52.two_hbm, bf16[256,2048]{1,0:T(8,128)(2,1)} %go_ref.1, ...), custom_call_target="tpu_custom_call" | custom-call | flops 60000002048 | bytes 550000000 | tf_op jit(solution)/shard_map/pallas_call | solution.py:314
  484.6 0.0 reduce-scatter.5.cloned.1.call-update
  484.7 73.1 %shard_map.216 = (f32[256,2048]{1,0:T(8,128)}, f32[16,256]{1,0:T(8,128)}) custom-call(bf16[4,256,2048]{2,1,0:T(8,128)(2,1)} %get-tuple-element.64.part_hbm, bf16[4,256,2048]{2,1,0:T(8,128)(2,1)} %get-tuple-element.47.normed_hbm.other_hbm, bf16[256,2048]{1,0:T(8,128)(2,1)} %tokens_hbm.3, f32[256,2048]{1,0:T(8,128)} %get-tuple-element.65.grads_hbm, ...), custom_call_target="tpu_custom_call" | custom-call | bytes 270000000 | tf_op jit(solution)/shard_map/pallas_call | solution.py:561
  557.8 0.0 reduce-scatter.3.cloned.1.call-done.gate_in.up_in.down_in
  557.8 6.9 %shard_map.217 = (f32[256,2048]{1,0:T(8,128)}, f32[256,2048]{1,0:T(8,128)}, f32[2048,256]{1,0:T(8,128)}, f32[256,2048]{1,0:T(8,128)}, bf16[256,2048]{1,0:T(8,128)(2,1)}, /*index=5*/f32[2,256]{1,0:T(2,128)}) custom-call(bf16[256,6144]{1,0:T(8,128)(2,1)} %reduce-scatter.3.cloned.1.call-done.gate_in.up_in.down_in, ...), custom_call_target="tpu_custom_call" | custom-call | tf_op jit(solution)/shard_map/pallas_call | solution.py:884
  564.7 0.0 reduce-scatter.5.cloned.1.call-done.mix_ref
  564.8 2.2 shard_map.218
  (4 shorter events, 0.0 us)
Async XLA Ops:
  7.2 3.4 copy-start.1
  7.2 3.4 copy-start.2
  7.2 3.5 copy-start
  7.2 82.5 %all-gather.7.cloned.1.call-start = ((), (), s32[]{:S(2)}) async-start(), calls=%async_computation.3 | async-start | bytes 2359296 | tf_op jit(solution)/shard_map/all_gather | solution.py:963
  7.9 81.8 %all-gather.5.cloned.1.call-start = ((), (), s32[]{:S(2)}) async-start(), calls=%async_computation.2 | async-start | bytes 3538944 | tf_op jit(solution)/shard_map/all_gather | solution.py:962
  9.8 220.0 %all-gather.11.cloned.1.call-start = ((), (), s32[]{:S(2)}) async-start(), calls=%async_computation.5 | async-start | bytes 9437184 | tf_op jit(solution)/shard_map/all_gather | solution.py:964
  10.6 219.3 %all-gather.9.cloned.1.call-start = ((), (), s32[]{:S(2)}) async-start(), calls=%async_computation.4 | async-start | bytes 18874368 | tf_op jit(solution)/shard_map/all_gather | solution.py:969
  89.7 468.1 %reduce-scatter.3.cloned.1.call-start = ((), (), s32[]{:S(2)}) async-start(), calls=%async_computation.6 | async-start | bytes 28311552 | tf_op jit(solution)/shard_map/reduce_scatter | solution.py:976
  334.0 230.7 %reduce-scatter.5.cloned.1.call-start = ((), (), s32[]{:S(2)}) async-start(), calls=%async_computation.7 | async-start | bytes 5898240 | tf_op jit(solution)/shard_map/reduce_scatter | solution.py:981
Sparse Core Ops, SparseCore 0:
  9.9 30.8 all-gather.6
  43.3 32.3 all-gather.4
  77.5 55.9 all-gather.10
  135.3 89.8 all-gather.8
  334.1 157.6 reduce-scatter.2
  495.1 57.2 reduce-scatter.4
